TPU v7x, 32 devices: a whole 2x2x4 slice. The times are simulated.
32 devices in a mesh: fsdp: 16 (over z, x, core), tp: 2 (over y).
Axes of the slice: x: 2, y: 2, z: 4, core: 2. Of those that a mesh axis runs over, the one named last changes fastest.
Arguments:
- tokens: bfloat16 [64, 256, 768], P('fsdp', 'tp'), may hold values from -6 to 6
- cotangent: bfloat16 [64, 256, 768], P('fsdp', 'tp'), may hold values from -6 to 6
- image_counts: int32 [16], P('fsdp'), may hold values from 2 to 4, as said below
- split_points: int32 [64], P('fsdp'), may hold values from 69 to 128, as said below
- attend_gain: bfloat16 [768], P('fsdp'), may hold values from 0.5 to 1.5
- attend_shift: bfloat16 [768], P('fsdp'), may hold values from -3 to 3
- qkv_weight: bfloat16 [768, 3, 768], P('fsdp', None, 'tp'), may hold values from -0.21875 to 0.21875
- query_value_bias: bfloat16 [2, 768], P(None, ('tp', 'fsdp')), may hold values from -3 to 3
- output_weight: bfloat16 [768, 768], P('tp', 'fsdp'), may hold values from -0.875 to 0.875
- output_bias: bfloat16 [768], P('fsdp'), may hold values from -3 to 3
- dense_gain: bfloat16 [768], P('fsdp'), may hold values from 0.5 to 1.5
- dense_shift: bfloat16 [768], P('fsdp'), may hold values from -3 to 3
- up_weight: bfloat16 [768, 3072], P('fsdp', 'tp'), may hold values from -0.21875 to 0.21875
- up_bias: bfloat16 [3072], P(('tp', 'fsdp')), may hold values from -3 to 3
- down_weight: bfloat16 [3072, 768], P('tp', 'fsdp'), may hold values from -0.109375 to 0.109375
- down_bias: bfloat16 [768], P('fsdp'), may hold values from -3 to 3
Outputs:
- out_tokens: bfloat16 [64, 256, 768], P('fsdp', 'tp')
- grad_tokens: float32 [64, 256, 768], P('fsdp', 'tp')
- grad_attend_gain: float32 [768], P('fsdp')
- grad_attend_shift: float32 [768], P('fsdp')
- grad_qkv_weight: float32 [768, 3, 768], P('fsdp', None, 'tp')
- grad_query_value_bias: float32 [2, 768], P(None, ('tp', 'fsdp'))
- grad_output_weight: float32 [768, 768], P('tp', 'fsdp')
- grad_output_bias: float32 [768], P('fsdp')
- grad_dense_gain: float32 [768], P('fsdp')
- grad_dense_shift: float32 [768], P('fsdp')
- grad_up_weight: float32 [768, 3072], P('fsdp', 'tp')
- grad_up_bias: float32 [3072], P(('tp', 'fsdp'))
- grad_down_weight: float32 [3072, 768], P('tp', 'fsdp')
- grad_down_bias: float32 [768], P('fsdp')
Inputs may be any that keep to these rules, and one draw needn't show every extreme that they name: image_counts[f] live images fill the first image slots of fsdp index f; some index has all 4 live. `split_points`: some image has 128 tokens in its first half and some has 69.
All inputs are finite; a program needn't handle non-finite values.
Results may differ from a plain program's by a relative error of at most 0.015.
Values may be sent and summed in bfloat16 or wider, within the bound.
No kernel may reach another device: no remote copies, remote signals or barrier semaphores. Data moves between devices by JAX's collectives and lax.ppermute only.
A program may use at most 128 MiB of HBM per device.

v0:
```python
from functools import partial
import math

import jax
import jax.numpy as jnp
from jax import lax
from jax.experimental import pallas as pl
from jax.experimental.pallas import tpu as pltpu
from jax.sharding import PartitionSpec as P

HD = 64
PAIR = 2 * HD
SEQ = 197

norm_epsilon = 1e-06
masked_score = -1e30
f32 = jnp.float32
bf16 = jnp.bfloat16


def dot(left, right):
    return jnp.dot(left, right, preferred_element_type=f32)


def dot_nt(left, right):
    return lax.dot_general(left, right, (((1,), (1,)), ((), ())), preferred_element_type=f32)


def dot_tn(left, right):
    return lax.dot_general(left, right, (((0,), (0,)), ((), ())), preferred_element_type=f32)


def mean_of(values):
    return jnp.mean(values, axis=-1, keepdims=True)


def normal_parts(values):
    centre = values - mean_of(values)
    rate = lax.rsqrt(mean_of(centre * centre) + norm_epsilon)
    return centre * rate, rate


def normal_back(normal, rate, norm_gain, grad):
    scaled = grad * norm_gain
    return rate * (scaled - mean_of(scaled) - normal * mean_of(scaled * normal))


def column_sum(values):
    return jnp.sum(values, axis=0, keepdims=True)


def head_masks():
    lane = lax.broadcasted_iota(jnp.int32, (1, PAIR), 1)
    first = (lane < HD).astype(f32)
    return first, 1.0 - first


def both_heads(slab, first, second):
    return jnp.concatenate([slab * first.astype(bf16), slab * second.astype(bf16)], axis=0)


def one_of_each(stacked, first, second):
    size = stacked.shape[0] // 2
    return stacked[:size] * first + stacked[size:] * second


def join_cores(core_ref, own_ref, swapped_ref, whole_ref):
    @pl.when(core_ref[0] == 0)
    def _():
        whole_ref[:, 0] = own_ref[...]
        whole_ref[:, 1] = swapped_ref[...]

    @pl.when(core_ref[0] != 0)
    def _():
        whole_ref[:, 0] = swapped_ref[...]
        whole_ref[:, 1] = own_ref[...]


class Fetch:
    def __init__(self, core_ref, own_ref, swapped_ref, whole_ref, sems, at):
        place = core_ref[0]
        self.copies = [
            pltpu.make_async_copy(own_ref, whole_ref.at[:, place], sems.at[at]),
            pltpu.make_async_copy(swapped_ref, whole_ref.at[:, 1 - place], sems.at[at + 1]),
        ]
        for copy in self.copies:
            copy.start()

    def wait(self):
        for copy in self.copies:
            copy.wait()


def flat(value):
    return value.reshape(-1, value.shape[-1])


def split_cores(core_ref, value, kept_ref, sent_ref, columns):
    blocks, rows, _ = kept_ref.shape
    value = value.astype(bf16).reshape(blocks, 2, rows, value.shape[-1])

    @pl.when(core_ref[0] == 0)
    def _():
        kept_ref[:, :, columns] = value[:, 0]
        sent_ref[:, :, columns] = value[:, 1]

    @pl.when(core_ref[0] != 0)
    def _():
        kept_ref[:, :, columns] = value[:, 1]
        sent_ref[:, :, columns] = value[:, 0]


def row_mask(bounds_ref, image, slot_count):
    place = lax.broadcasted_iota(jnp.int32, (slot_count, 1), 0)
    return jnp.concatenate(
        [(place < bounds_ref[image, 2 + part]).astype(f32) for part in range(2)], axis=0
    )


def owner_of(size, each, fsdp):
    column = lax.broadcasted_iota(jnp.int32, (fsdp, size), 1)
    start = lax.broadcasted_iota(jnp.int32, (fsdp, size), 0) * each
    held = ((column >= start) & (column < start + each)).astype(f32)
    return held, jnp.sum(held * start.astype(f32), axis=0, keepdims=True)


def place_of(size, start_row, offset):
    lane = lax.broadcasted_iota(jnp.int32, (128, size), 0).astype(f32)
    column = lax.broadcasted_iota(jnp.int32, (128, size), 1).astype(f32)
    return (column - start_row + offset == lane).astype(f32)


def row_picker(start, count, fsdp, rows):
    width = fsdp * rows
    place = lax.broadcasted_iota(jnp.int32, (fsdp, width), 1) - rows * lax.broadcasted_iota(
        jnp.int32, (fsdp, width), 0
    )
    picked = [(place == i).astype(f32) for i in range(start, start + count)]
    return jnp.concatenate(picked, axis=0).astype(bf16)


def small_groups(rows):
    return [range(at, min(at + rows, 8)) for at in range(0, 8, rows)]


def lay_out(shards, size, each, offset):
    held, start_row = owner_of(size, each, shards.shape[0])
    placed = dot(shards.astype(bf16), place_of(size, start_row, offset).astype(bf16))
    return column_sum(placed * held)


def take_apart(row, fsdp, each, offset):
    size = row.shape[1]
    held, start_row = owner_of(size, each, fsdp)
    return dot_nt((held * row).astype(bf16), place_of(size, start_row, offset).astype(bf16))


def attend_forward_kernel(image, made, fsdp, *refs):
    core_ref, bounds_ref, own_ref, other_ref = refs[:4]
    one_ref, one_swapped_ref, two_ref, two_swapped_ref = refs[4:8]
    refs, sems = refs[8 if made else 14 : -1], refs[-1]
    first_ref, joint_ref, chances_ref, mixed_ref, middle_ref, second_ref = refs[:6]
    up_add_ref, vec_ref, one_whole, two_whole = refs[-4:] if made else (None, *refs[-3:])
    slot_count, width = own_ref.shape[1:]
    half = width // 2
    each = width // fsdp
    stride = two_whole.shape[-1] // 2
    two_fetch = Fetch(core_ref, two_ref, two_swapped_ref, two_whole, sems, 2)
    one_fetch = Fetch(core_ref, one_ref, one_swapped_ref, one_whole, sems, 0)
    inputs = jnp.concatenate([own_ref[0], other_ref[0]], axis=0).astype(f32)
    normal, _ = normal_parts(inputs)
    two_fetch.wait()
    small = []
    for y in range(2):
        base = y * stride + 2 * half
        found = []
        for block, group in enumerate(small_groups(each)):
            columns = flat(two_whole[:, :, :, base + block * 128 : base + (block + 1) * 128])
            picked = dot(row_picker(0, len(group), fsdp, each), columns)
            found += [picked[i * fsdp : (i + 1) * fsdp] for i in range(len(group))]
        small.append(found)
    for i in range(6):
        vec_ref[i : i + 1] = lay_out(small[0][i], width, each, 0)
    for y in range(2):
        for i in range(2):
            vec_ref[6 + i : 7 + i, y * half : (y + 1) * half] = lay_out(
                small[y][6], half, each // 2, i * (each // 2)
            )
    if made:
        parts, part_size = up_add_ref.shape
        piece = part_size // 2
        for y in range(2):
            row = lay_out(small[y][7], parts * piece, 2 * each, 0)
            for i in range(parts):
                up_add_ref[i : i + 1, y * piece : (y + 1) * piece] = row[
                    :, i * piece : (i + 1) * piece
                ]
    one_fetch.wait()
    first_rows = (normal * vec_ref[0:1] + vec_ref[1:2]).astype(bf16)
    first_ref[0] = first_rows
    for y in range(2):
        at = y * half
        here = slice(at, at + half)
        base = y * 2 * half
        query = dot(first_rows, flat(one_whole[:, :, :, base : base + half])) + vec_ref[6:7, here]
        key = dot(first_rows, flat(one_whole[:, :, :, base + half : base + 2 * half]))
        after = y * stride
        value = dot(first_rows, flat(two_whole[:, :, :, after : after + half])) + vec_ref[7:8, here]
        joint_ref[0, :, at : at + half] = (query.astype(bf16).astype(f32) * HD ** (-0.5)).astype(bf16)
        joint_ref[0, :, width + at : width + at + half] = key.astype(bf16)
        joint_ref[0, :, 2 * width + at : 2 * width + at + half] = value.astype(bf16)
    place = lax.broadcasted_iota(jnp.int32, (1, slot_count), 1)
    live = jnp.concatenate(
        [(place < bounds_ref[image, part]).astype(jnp.int32) for part in range(2)], axis=1
    )
    first, second = head_masks()
    for pair in range(width // PAIR):
        at = pair * PAIR
        query = both_heads(joint_ref[0, :, at : at + PAIR], first, second)
        key = joint_ref[0, :, width + at : width + at + PAIR]
        value = joint_ref[0, :, 2 * width + at : 2 * width + at + PAIR]
        scores = jnp.where(live > 0, dot_nt(query, key), masked_score)
        raised = jnp.exp(scores - jnp.max(scores, axis=-1, keepdims=True))
        chances = (raised / jnp.sum(raised, axis=-1, keepdims=True)).astype(bf16)
        chances_ref[0, pair] = chances
        mixed_ref[0, :, at : at + PAIR] = one_of_each(dot(chances, value), first, second).astype(
            bf16
        )
    middle = inputs + vec_ref[2:3]
    for y in range(2):
        base = y * stride + half
        middle += dot_nt(
            mixed_ref[0, :, y * half : (y + 1) * half],
            flat(two_whole[:, :, :, base : base + half]),
        )
    middle_ref[0] = middle
    normal, _ = normal_parts(middle)
    second_ref[0] = (normal * vec_ref[3:4] + vec_ref[4:5]).astype(bf16)


def masked_grads(bounds_ref, own_ref, other_ref, image):
    grads = jnp.concatenate([own_ref[image], other_ref[image]], axis=0).astype(f32)
    return grads * row_mask(bounds_ref, image, own_ref.shape[1])


def dense_up_kernel(
    core_ref,
    bounds_ref,
    second_ref,
    own_ref,
    other_ref,
    up_ref,
    up_swapped_ref,
    up_add_ref,
    active_ref,
    slope_ref,
    kept_ref,
    sent_ref,
    up_whole,
    grad_in,
):
    images, slot_count, _ = own_ref.shape
    length = 2 * slot_count

    @pl.when(pl.program_id(0) == 0)
    def _():
        for image in range(images):
            rows = slice(image * length, (image + 1) * length)
            grad_in[rows] = masked_grads(bounds_ref, own_ref, other_ref, image).astype(bf16)

    join_cores(core_ref, up_ref, up_swapped_ref, up_whole)
    hidden = dot(second_ref[...], flat(up_whole[...])) + up_add_ref[...]
    below = 0.5 * (1.0 + lax.erf(hidden * math.sqrt(0.5)))
    density = jnp.exp(-0.5 * hidden * hidden) * (1.0 / math.sqrt(2.0 * math.pi))
    active = (hidden * below).astype(bf16)
    active_ref[...] = active
    slope_ref[...] = (below + hidden * density).astype(bf16)
    split_cores(core_ref, dot_tn(grad_in[...], active), kept_ref, sent_ref, slice(None))


def dense_down_kernel(opening, *refs):
    core_ref, bounds_ref, own_ref, other_ref, second_ref, active_ref, slope_ref = refs[:7]
    up_ref, up_swapped_ref, down_ref, down_swapped_ref = refs[7:11]
    refs = refs[11:]
    if opening:
        kept_ref, sent_ref, up_sums_ref, out_total, back_total = refs[:5]
    else:
        middle_ref, vec_ref, out_before_ref, back_before_ref = refs[:4]
        kept_ref, sent_ref, up_sums_ref = refs[4:7]
        out_own_ref, out_other_ref, grad_middle_ref, sums_ref = refs[7:11]
        out_total, back_total = refs[-2:]
    up_whole, down_whole, grad_in = refs[5:8] if opening else refs[11:14]
    step = pl.program_id(0)
    images, slot_count, _ = own_ref.shape
    length = 2 * slot_count

    @pl.when(step == 0)
    def _():
        for image in range(images):
            rows = slice(image * length, (image + 1) * length)
            grad_in[rows] = masked_grads(bounds_ref, own_ref, other_ref, image).astype(bf16)
        if opening:
            out_total[...] = jnp.zeros_like(out_total)
            back_total[...] = jnp.zeros_like(back_total)
        else:
            out_total[...] = out_before_ref[...]
            back_total[...] = back_before_ref[...]

    join_cores(core_ref, up_ref, up_swapped_ref, up_whole)
    join_cores(core_ref, down_ref, down_swapped_ref, down_whole)
    up = flat(up_whole[...])
    down = flat(down_whole[...])
    grad_hidden = (dot(grad_in[...], down) * slope_ref[...].astype(f32)).astype(bf16)
    split_cores(core_ref, dot_tn(second_ref[...], grad_hidden), kept_ref, sent_ref, slice(None))
    up_sums_ref[...] = column_sum(grad_hidden.astype(f32))
    out_total[...] += dot_nt(active_ref[...], down)
    back_total[...] += dot_nt(grad_hidden, up)
    if opening:
        return

    @pl.when(step == pl.num_programs(0) - 1)
    def _():
        sums = [0.0] * 4
        for image in range(images):
            rows = slice(image * length, (image + 1) * length)
            middle = middle_ref[rows]
            result = (middle + out_total[rows] + vec_ref[5:6]) * row_mask(
                bounds_ref, image, slot_count
            )
            result = result.astype(bf16)
            out_own_ref[image] = result[:slot_count]
            out_other_ref[image] = result[slot_count:]
            grads = masked_grads(bounds_ref, own_ref, other_ref, image)
            back = back_total[rows].astype(bf16).astype(f32)
            normal, rate = normal_parts(middle)
            grad_middle = grads + normal_back(normal, rate, vec_ref[3:4], back)
            grad_middle_ref[rows] = grad_middle
            for i, term in enumerate((grad_middle, back * normal, back, grads)):
                sums[i] += column_sum(term)
        for i in range(4):
            sums_ref[i : i + 1] = sums[i]


def attend_backward_kernel(*refs):
    core_ref, own_ref, other_ref, grad_middle_ref, joint_ref, chances_ref = refs[:6]
    one_ref, one_swapped_ref, two_ref, two_swapped_ref, vec_ref = refs[6:11]
    grad_joint_ref, grad_own_ref, grad_other_ref, sums_ref = refs[-7:-3]
    one_whole, two_whole, sems = refs[-3:]
    slot_count, width = own_ref.shape[1:]
    half = width // 2
    stride = two_whole.shape[-1] // 2
    two_fetch = Fetch(core_ref, two_ref, two_swapped_ref, two_whole, sems, 2)
    one_fetch = Fetch(core_ref, one_ref, one_swapped_ref, one_whole, sems, 0)
    first, second = head_masks()
    length = 2 * slot_count
    grad_middle = grad_middle_ref[...]
    branch = grad_middle.astype(bf16)
    two_fetch.wait()
    grad_mixed = jnp.concatenate(
        [dot(branch, flat(two_whole[:, :, :, base : base + half])) for base in (half, stride + half)],
        axis=1,
    ).astype(bf16)
    for pair in range(width // PAIR):
        at = pair * PAIR
        query = both_heads(joint_ref[0, :, at : at + PAIR], first, second)
        key = joint_ref[0, :, width + at : width + at + PAIR]
        value = joint_ref[0, :, 2 * width + at : 2 * width + at + PAIR]
        grad_pair = both_heads(grad_mixed[:, at : at + PAIR], first, second)
        chances = chances_ref[0, pair]
        grad_value = dot_tn(chances, grad_pair)
        wide = chances.astype(f32)
        weighted = wide * dot_nt(grad_pair, value)
        grad_scores = (weighted - wide * jnp.sum(weighted, axis=-1, keepdims=True)).astype(bf16)
        grad_query = one_of_each(dot(grad_scores, key), first, second) * HD ** (-0.5)
        grad_key = dot_tn(grad_scores, query)
        grad_joint_ref[0, :, at : at + PAIR] = grad_query.astype(bf16)
        grad_joint_ref[0, :, width + at : width + at + PAIR] = grad_key.astype(bf16)
        grad_joint_ref[0, :, 2 * width + at : 2 * width + at + PAIR] = grad_value.astype(bf16)
    one_fetch.wait()
    back = jnp.zeros((length, width), f32)
    for y in range(2):
        at = y * half
        base = y * 2 * half
        for part, matrix in (
            (0, one_whole[:, :, :, base : base + half]),
            (1, one_whole[:, :, :, base + half : base + 2 * half]),
            (2, two_whole[:, :, :, y * stride : y * stride + half]),
        ):
            columns = slice(part * width + at, part * width + at + half)
            back += dot_nt(grad_joint_ref[0, :, columns], flat(matrix))
    back = back.astype(bf16).astype(f32)
    inputs = jnp.concatenate([own_ref[0], other_ref[0]], axis=0).astype(f32)
    normal, rate = normal_parts(inputs)
    grad_tokens = grad_middle + normal_back(normal, rate, vec_ref[0:1], back)
    grad_own_ref[0] = grad_tokens[:slot_count]
    grad_other_ref[0] = grad_tokens[slot_count:].astype(bf16)
    sums_ref[0, 0:1] = column_sum(back * normal)
    sums_ref[0, 1:2] = column_sum(back)
    sums_ref[0, 2:3] = column_sum(grad_joint_ref[0, :, :width].astype(f32))
    sums_ref[0, 3:4] = column_sum(grad_joint_ref[0, :, 2 * width :].astype(f32))


def attend_weights_kernel(
    fsdp,
    core_ref,
    grad_middle_ref,
    first_ref,
    mixed_ref,
    grad_joint_ref,
    sums_ref,
    dense_sums_ref,
    up_sums_ref,
    one_kept_ref,
    one_sent_ref,
    two_kept_ref,
    two_sent_ref,
):
    total, width = grad_middle_ref.shape
    half = width // 2
    stride = two_kept_ref.shape[-1] // 2
    first_rows = first_ref[...]
    branch = grad_middle_ref[...].astype(bf16)
    for y in range(2):
        at = y * half
        base = y * 2 * half
        here = slice(base, base + half)
        after = slice(base + half, base + 2 * half)
        for part, kept, sent, columns in (
            (0, one_kept_ref, one_sent_ref, here),
            (1, one_kept_ref, one_sent_ref, after),
            (2, two_kept_ref, two_sent_ref, slice(y * stride, y * stride + half)),
        ):
            start = part * width + at
            grad = dot_tn(first_rows, grad_joint_ref[:, start : start + half])
            split_cores(core_ref, grad, kept, sent, columns)
        grad = dot_tn(branch, mixed_ref[:, at : at + half])
        after = slice(y * stride + half, y * stride + 2 * half)
        split_cores(core_ref, grad, two_kept_ref, two_sent_ref, after)
    each = width // fsdp
    sums = [sums_ref[0, i : i + 1] + sums_ref[1, i : i + 1] for i in range(4)]
    plain = sums[:2] + [dense_sums_ref[i : i + 1] for i in range(4)]
    plain = [take_apart(row, fsdp, each, 0) for row in plain]
    parts, part_size = up_sums_ref.shape
    piece = part_size // 2
    for y in range(2):
        here = slice(y * half, (y + 1) * half)
        joint_apart = take_apart(sums[2][:, here], fsdp, each // 2, 0)
        joint_apart += take_apart(sums[3][:, here], fsdp, each // 2, each // 2)
        row = jnp.concatenate(
            [up_sums_ref[i : i + 1, y * piece : (y + 1) * piece] for i in range(parts)], axis=1
        )
        apart = plain + [joint_apart, take_apart(row, fsdp, 2 * each, 0)]
        for block, group in enumerate(small_groups(each)):
            stacked = jnp.concatenate([apart[i] for i in group], axis=0).astype(bf16)
            grad = dot_tn(row_picker(0, len(group), fsdp, each), stacked)
            start = y * stride + 2 * half + block * 128
            split_cores(core_ref, grad, two_kept_ref, two_sent_ref, slice(start, start + 128))


def ordered(kernel, start, count, scratch):
    def run(*refs):
        refs = refs[:start] + refs[start + count :]
        last = len(refs) - scratch - 1
        kernel(*refs[:last], *refs[last + 1 :])
        refs[last][0] = 0

    return run


in_smem = pl.BlockSpec(memory_space=pltpu.SMEM)
in_vmem = pl.BlockSpec(memory_space=pltpu.VMEM)
anywhere = pl.BlockSpec(memory_space=pl.ANY)


def fixed(array):
    return pl.BlockSpec(array.shape, lambda *_: (0,) * len(array.shape))


def per_step(shape, axis):
    return pl.BlockSpec(shape, lambda step: tuple(step if i == axis else 0 for i in range(len(shape))))


def block_at(shape, index):
    return pl.BlockSpec(shape, lambda step: (index,) + (0,) * (len(shape) - 1))


def params(mebibytes):
    return pltpu.CompilerParams(vmem_limit_bytes=mebibytes * 1024 * 1024)


def cost(microseconds=0.1):
    return pl.CostEstimate(
        flops=int(microseconds * 1e9), bytes_accessed=100_000, transcendentals=0
    )


def out(shape, kind):
    return jax.ShapeDtypeStruct(shape, kind)


def far_out(shape, kind):
    return pltpu.HBM(shape, kind)


def core_scratch(array, columns=None):
    blocks, rows, own_columns = array.shape
    return pltpu.VMEM((blocks, 2, rows, columns or own_columns), bf16)


token = out((1,), jnp.int32)


def attend_forward(
    image, core, bounds, own, other, one, two, fsdp, parts, hidden, before, earlier
):
    images, slot_count, width = own.shape
    length = 2 * slot_count
    pairs = width // PAIR
    made = before is None
    shapes = [
        ((images, length, width), bf16),
        ((images, length, 3 * width), bf16),
        ((images, pairs, 2 * length, length), bf16),
        ((images, length, width), bf16),
        ((images, length, width), f32),
        ((images, length, width), bf16),
    ]
    out_shape = [far_out(*shape) for shape in shapes]
    out_specs = [block_at((1,) + shape[1:], image) for shape, _ in shapes]
    vec = out((8, width), f32)
    if made:
        add = out((parts, hidden // parts), f32)
        out_shape += [add, vec]
        out_specs += [fixed(add), fixed(vec)]
    out_shape.append(token)
    out_specs.append(in_smem)
    return pl.pallas_call(
        ordered(
            partial(attend_forward_kernel, image, made, fsdp),
            8 if made else 14,
            len(earlier),
            3 if made else 4,
        ),
        grid=(1,),
        in_specs=[
            in_smem,
            in_smem,
            block_at((1, slot_count, width), image),
            block_at((1, slot_count, width), image),
            *([anywhere] * 4),
            *([] if made else [anywhere] * 6),
            *([anywhere] * len(earlier)),
        ],
        out_specs=out_specs,
        out_shape=out_shape,
        scratch_shapes=[
            *([] if made else [pltpu.VMEM(vec.shape, f32)]),
            core_scratch(one[0]),
            core_scratch(two[0]),
            pltpu.SemaphoreType.DMA((4,)),
        ],
        input_output_aliases={} if made else {8 + i: i for i in range(6)},
        compiler_params=params(21),
        cost_estimate=cost(9),
        name="attend_forward",
    )(core, bounds, own, other, *one, *two, *([] if made else before), *earlier)


def dense_up(core, bounds, second, own, other, up, up_add, tile, earlier):
    total, width = second.shape
    blocks, rows, columns = up[0].shape
    weights = per_step((blocks, rows, tile), 2)
    return pl.pallas_call(
        ordered(dense_up_kernel, 8, len(earlier), 2),
        grid=(columns // tile,),
        in_specs=[
            in_smem,
            in_smem,
            fixed(second),
            fixed(own),
            fixed(other),
            weights,
            weights,
            per_step((1, tile), 1),
            *([anywhere] * len(earlier)),
        ],
        out_specs=[per_step((total, tile), 1)] * 2 + [weights, weights, in_smem],
        out_shape=[
            far_out((total, columns), bf16),
            far_out((total, columns), bf16),
            out(up[0].shape, bf16),
            out(up[0].shape, bf16),
            token,
        ],
        scratch_shapes=[core_scratch(up[0], tile), pltpu.VMEM((total, width), bf16)],
        compiler_params=params(13),
        cost_estimate=cost(8),
        name="dense_up",
    )(core, bounds, second, own, other, *up, up_add, *earlier)


def dense_down(core, bounds, own, other, second, active, slope, up, down, tile, before, earlier):
    total, width = second.shape
    blocks, rows, columns = up[0].shape
    opening = before is None
    weights = per_step((blocks, rows, tile), 2)
    whole = pl.BlockSpec((total, width), lambda step: (0, 0))
    sums = pl.BlockSpec((8, width), lambda step: (0, 0))
    part_shape = far_out((total, width), f32)
    if opening:
        more_shapes, more_specs = [part_shape] * 2, [whole] * 2
    else:
        more_shapes = [out(own.shape, bf16)] * 2 + [part_shape, out((8, width), f32)]
        more_specs = [fixed(own), fixed(own), whole, sums]
    return pl.pallas_call(
        ordered(
            partial(dense_down_kernel, opening),
            11 if opening else 15,
            len(earlier),
            3 if opening else 5,
        ),
        grid=(columns // tile,),
        in_specs=[
            in_smem,
            in_smem,
            fixed(own),
            fixed(other),
            whole,
            per_step((total, tile), 1),
            per_step((total, tile), 1),
            *([weights] * 4),
            *([] if opening else [whole, sums, whole, whole]),
            *([anywhere] * len(earlier)),
        ],
        out_specs=[weights, weights, per_step((1, tile), 1)] + more_specs + [in_smem],
        out_shape=[
            out(up[0].shape, bf16),
            out(up[0].shape, bf16),
            out((1, columns), f32),
        ]
        + more_shapes
        + [token],
        scratch_shapes=[
            core_scratch(up[0], tile),
            core_scratch(up[0], tile),
            pltpu.VMEM((total, width), bf16),
            *([] if opening else [pltpu.VMEM((total, width), f32)] * 2),
        ],
        compiler_params=params(20 if opening else 31),
        cost_estimate=cost(12),
        name="dense_down",
    )(
        core,
        bounds,
        own,
        other,
        second,
        active,
        slope,
        *up,
        *down,
        *([] if opening else before),
        *earlier,
    )


def attend_backward(
    image, core, own, other, grad_middle, joint, chances, one, two, vec, before, earlier
):
    images, slot_count, width = own.shape
    length = 2 * slot_count
    rows = block_at((1, slot_count, width), image)
    outs = [
        ((images, length, 3 * width), bf16),
        ((images, slot_count, width), f32),
        ((images, slot_count, width), bf16),
        ((images, 8, width), f32),
    ]
    return pl.pallas_call(
        ordered(attend_backward_kernel, 11 + len(before), len(earlier), 3),
        grid=(1,),
        in_specs=[
            in_smem,
            rows,
            rows,
            block_at((length, width), image),
            block_at((1,) + joint.shape[1:], image),
            block_at((1,) + chances.shape[1:], image),
            *([anywhere] * 4),
            fixed(vec),
            *([anywhere] * (len(before) + len(earlier))),
        ],
        out_specs=[block_at((1,) + shape[1:], image) for shape, _ in outs] + [in_smem],
        out_shape=[far_out(*outs[0])] + [out(*each) for each in outs[1:]] + [token],
        scratch_shapes=[
            core_scratch(one[0]),
            core_scratch(two[0]),
            pltpu.SemaphoreType.DMA((4,)),
        ],
        input_output_aliases={11 + i: i for i in range(len(before))},
        compiler_params=params(24),
        cost_estimate=cost(10),
        name="attend_backward",
    )(core, own, other, grad_middle, joint, chances, *one, *two, vec, *before, *earlier)


def attend_weights(
    fsdp, core, grad_middle, first, mixed, grad_joint, sums, dense_sums, up_sums, one, two, earlier
):
    arrays = [core, grad_middle, first, mixed, grad_joint, sums, dense_sums, up_sums]
    outs = [out(pair[0].shape, bf16) for pair in (one, one, two, two)]
    return pl.pallas_call(
        ordered(partial(attend_weights_kernel, fsdp), len(arrays), len(earlier), 0),
        in_specs=[in_smem] + [in_vmem] * 7 + [anywhere] * len(earlier),
        out_specs=[in_vmem] * 4 + [in_smem],
        out_shape=outs + [token],
        compiler_params=params(28),
        cost_estimate=cost(6),
        name="attend_weights",
    )(*arrays, *earlier)


def at_side(ref, kind, side):
    if kind == "x":
        return ref.at[:, side]
    size = ref.shape[-1] // 2
    return ref.at[:, :, pl.ds(pl.multiple_of(side * size, 128), size)]


def joined_shape(array, kind):
    if kind == "x":
        return (array.shape[0], 2) + array.shape[1:]
    return array.shape[:-1] + (2 * array.shape[-1],)


def take_rows_kernel(side_ref, *refs):
    count = len(refs) // 2
    for i in range(count):
        refs[count + i][...] = refs[i][...]


def take_rows(side, arrays):
    shapes = [(array.shape[0] // 2,) + array.shape[1:] for array in arrays]
    return pl.pallas_call(
        take_rows_kernel,
        grid_spec=pltpu.PrefetchScalarGridSpec(
            num_scalar_prefetch=1,
            grid=(1,),
            in_specs=[pl.BlockSpec(shape, lambda step, side: (side[0], 0, 0)) for shape in shapes],
            out_specs=[pl.BlockSpec(shape, lambda step, side: (0, 0, 0)) for shape in shapes],
        ),
        out_shape=[out(shape, bf16) for shape in shapes],
        compiler_params=params(8),
        cost_estimate=cost(),
        name="take_rows",
    )(side, *arrays)


def join_kernel(kinds, places, count, *refs):
    sides_ref, refs, token_ref = refs[0], refs[1:-1], refs[-1]
    token_ref[0] = 0
    pieces = len(kinds)
    ins, passed = refs[: 2 * pieces], refs[2 * pieces : 2 * pieces + count]
    outs = refs[len(refs) - pieces - count :]
    for i, kind in enumerate(kinds):
        side = sides_ref[places[i]]
        at_side(outs[i], kind, side)[...] = ins[2 * i][...]
        at_side(outs[i], kind, 1 - side)[...] = ins[2 * i + 1][...]
    for i in range(count):
        outs[pieces + i][...] = passed[i][...]


def join_pieces(sides, pieces, kinds, places, passed, earlier):
    outs = [out(joined_shape(own, kind), bf16) for (own, _), kind in zip(pieces, kinds)]
    outs += [out(array.shape, array.dtype) for array in passed]
    arrays = [array for pair in pieces for array in pair] + list(passed)
    return pl.pallas_call(
        partial(join_kernel, kinds, places, len(passed)),
        in_specs=[in_smem] + [in_vmem] * len(arrays) + [anywhere] * len(earlier),
        out_specs=[in_vmem] * len(outs) + [in_smem],
        out_shape=outs + [token],
        compiler_params=params(24),
        cost_estimate=cost(),
        name="join_pieces",
    )(sides, *arrays, *earlier)


def join_far_kernel(count, *refs):
    sides_ref, ins, passed = refs[0], refs[1:5], refs[5 : 5 + count]
    outs, token_ref = refs[len(refs) - 3 - count : -1], refs[-1]
    token_ref[0] = 0
    place = sides_ref[2]
    at = 0
    for ref in outs[:2]:
        size = ref.shape[-1]
        for mask in range(4):
            ref[:, place ^ mask] = ins[mask][:, :, at : at + size]
        at += size
    for i in range(count):
        outs[2 + i][...] = passed[i][...]


def join_far(sides, blocks, cut_at, passed, earlier):
    others, rows, columns = blocks[0].shape
    outs = [out((others, 4, rows, size), bf16) for size in (cut_at, columns - cut_at)]
    outs += [out(array.shape, array.dtype) for array in passed]
    return pl.pallas_call(
        partial(join_far_kernel, len(passed)),
        in_specs=[in_smem] + [in_vmem] * (4 + len(passed)) + [anywhere] * len(earlier),
        out_specs=[in_vmem] * len(outs) + [in_smem],
        out_shape=outs + [token],
        compiler_params=params(24),
        cost_estimate=cost(),
        name="join_far",
    )(sides, *blocks, *passed, *earlier)


def add_kernel(kinds, places, *refs):
    sides_ref, refs, token_ref = refs[0], refs[1:-1], refs[-1]
    token_ref[0] = 0
    pieces = len(kinds)
    ins, outs = refs[: 2 * pieces], refs[len(refs) - 2 * pieces :]
    for i, kind in enumerate(kinds):
        side = sides_ref[places[i]]
        for at, ref in ((side, outs[2 * i]), (1 - side, outs[2 * i + 1])):
            ref[...] = at_side(ins[2 * i], kind, at)[...] + at_side(ins[2 * i + 1], kind, at)[...]


def add_pieces(sides, pieces, kinds, places, earlier, microseconds):
    arrays, outs = [], []
    for pair, kind in zip(pieces, kinds):
        for array in pair:
            blocks, rows, columns = array.shape
            arrays.append(array.reshape(blocks // 2, 2, rows, columns) if kind == "x" else array)
        shape = (blocks // 2, rows, columns) if kind == "x" else (blocks, rows, columns // 2)
        outs += [out(shape, bf16)] * 2
    outs = pl.pallas_call(
        partial(add_kernel, kinds, places),
        in_specs=[in_smem] + [in_vmem] * len(arrays) + [anywhere] * len(earlier),
        out_specs=[in_vmem] * len(outs) + [in_smem],
        out_shape=outs + [token],
        compiler_params=params(24),
        cost_estimate=cost(microseconds),
        name="add_pieces",
    )(sides, *arrays, *earlier)
    return outs[0:-1:2], outs[1:-1:2], outs[-1]


def add_far_kernel(count, *refs):
    sides_ref, ins, passed, token_ref = refs[0], refs[1:5], refs[5 : 5 + count], refs[-1]
    token_ref[0] = 0
    refs = refs[:-1]
    outs = refs[len(refs) - 4 - count :]
    place = sides_ref[2]
    at = 0
    for kept, arrived in ((ins[0], ins[1]), (ins[2], ins[3])):
        size = kept.shape[-1]
        for mask in range(4):
            block = place ^ mask
            outs[mask][:, :, at : at + size] = kept[:, block] + arrived[:, block]
        at += size
    for i in range(count):
        outs[4 + i][...] = passed[i][...]


def add_far(sides, pieces, passed, earlier, microseconds):
    arrays = []
    for array in (array for pair in pieces for array in pair):
        blocks, rows, columns = array.shape
        arrays.append(array.reshape(blocks // 4, 4, rows, columns))
    width = pieces[0][0].shape[-1] + pieces[1][0].shape[-1]
    outs = [out((arrays[0].shape[0], rows, width), bf16)] * 4
    outs += [out(array.shape, array.dtype) for array in passed]
    return pl.pallas_call(
        partial(add_far_kernel, len(passed)),
        in_specs=[in_smem] + [in_vmem] * (4 + len(passed)) + [anywhere] * len(earlier),
        out_specs=[in_vmem] * len(outs) + [in_smem],
        out_shape=outs + [token],
        compiler_params=params(24),
        cost_estimate=cost(microseconds),
        name="add_far",
    )(sides, *arrays, *passed, *earlier)


def sum_far_kernel(*refs):
    total = refs[0][...].astype(f32)
    for ref in refs[1:4]:
        total += ref[...].astype(f32)
    refs[-2][...] = total
    refs[-1][0] = 0


def sum_far(blocks, earlier):
    return pl.pallas_call(
        sum_far_kernel,
        in_specs=[in_vmem] * 4 + [anywhere] * len(earlier),
        out_specs=[in_vmem, in_smem],
        out_shape=[out(blocks[0].shape, f32), token],
        compiler_params=params(24),
        cost_estimate=cost(),
        name="sum_far",
    )(*blocks, *earlier)


class Exchange:
    def __init__(self, fsdp, rows):
        self.fsdp = fsdp
        self.bits = fsdp.bit_length() - 1
        self.rows = rows
        self.f = lax.axis_index("fsdp")
        self.y = lax.axis_index("tp")
        self.sides = jnp.stack([self.side(1), self.y, (self.f >> 2) & 3]).astype(jnp.int32)
        self.apart = rows % 16 == 0
        self.core = (self.side(0) if self.apart else jnp.zeros((), jnp.int32)).reshape(1)

    def side(self, bit):
        return (self.f >> bit) & 1

    def swap(self, value, apart):
        if apart == "y":
            return lax.ppermute(value, "tp", [(0, 1), (1, 0)])
        apart = {"core": 1, "x": 2}.get(apart, apart)
        return lax.ppermute(value, "fsdp", [(i, i ^ apart) for i in range(self.fsdp)])

    def spread_bit(self, value, bit):
        other = self.swap(value, 1 << bit)
        first = self.side(bit) == 0
        return jnp.stack([jnp.where(first, value, other), jnp.where(first, other, value)])

    def start_far(self, shard):
        value = shard[None]
        for bit in range(4, self.bits):
            value = self.spread_bit(value, bit).reshape((-1,) + shard.shape)
        return (value, *(self.swap(value, mask << 2) for mask in (1, 2, 3)))

    def end_far(self, blocks, cut_at, passed=(), earlier=()):
        *pieces, mark = join_far(self.sides, blocks, cut_at, passed, earlier)
        joined = [piece.reshape(-1, self.rows, piece.shape[-1]) for piece in pieces[:2]]
        return joined, pieces[2:], mark

    def start(self, values, kinds):
        return [(value, self.swap(value, kind)) for value, kind in zip(values, kinds)]

    def end(self, pairs, kinds, passed=(), earlier=()):
        places = tuple("xy".index(kind) for kind in kinds)
        joined = join_pieces(self.sides, pairs, kinds, places, passed, earlier)
        flat_ones = [
            piece.reshape(-1, self.rows, piece.shape[-1]) for piece in joined[: len(kinds)]
        ]
        return flat_ones + list(joined[len(kinds) :])

    def both_cores(self, value):
        if self.apart:
            return value, self.swap(value, "core")
        other = self.swap(value, "core")
        first = self.side(0) == 0
        whole = jnp.stack(
            [jnp.where(first, value, other), jnp.where(first, other, value)], axis=1
        )
        whole = whole.reshape(-1, value.shape[-1])
        size = whole.shape[0] // 2
        return whole[None, :size], whole[None, size:]

    def start_cores(self, kept, sent):
        if not self.apart:
            whole = jnp.concatenate([kept[0], sent[0]], axis=0)
            whole = whole.reshape(-1, 2, self.rows, whole.shape[-1])
            kept = lax.dynamic_index_in_dim(whole, self.side(0), 1, keepdims=False)
            sent = lax.dynamic_index_in_dim(whole, 1 - self.side(0), 1, keepdims=False)
        return kept, self.swap(sent, "core")

    def add(self, pairs, kinds, earlier=(), microseconds=0.1):
        places = tuple("xy".index(kind) for kind in kinds)
        return add_pieces(self.sides, pairs, kinds, places, earlier, microseconds)

    def send(self, kept, sent, kinds):
        return [(value, self.swap(leaving, kind)) for value, leaving, kind in zip(kept, sent, kinds)]

    def add_far(self, pairs, passed=(), earlier=(), microseconds=0.1):
        *blocks, mark = add_far(self.sides, pairs, passed, earlier, microseconds)
        return blocks[:4], blocks[4:], mark

    def send_far(self, blocks):
        return (blocks[0], *(self.swap(blocks[mask], mask << 2) for mask in (1, 2, 3)))

    def sum_far(self, blocks, earlier=()):
        total, mark = sum_far(blocks, earlier)
        for bit in range(self.bits - 1, 3, -1):
            total = total.reshape((2, -1) + total.shape[1:])
            sent = lax.dynamic_index_in_dim(total, 1 - self.side(bit), 0, keepdims=False)
            kept = lax.dynamic_index_in_dim(total, self.side(bit), 0, keepdims=False)
            total = kept + self.swap(sent, 1 << bit)
        return total.reshape(self.rows, -1), mark


def on_device(
    fsdp,
    tokens,
    cotangent,
    image_counts,
    split_points,
    attend_gain,
    attend_shift,
    qkv_weight,
    query_value_bias,
    output_weight,
    output_bias,
    dense_gain,
    dense_shift,
    up_weight,
    up_bias,
    down_weight,
    down_bias,
):
    slots, slot_count, width = tokens.shape
    images = slots // 2
    rows = width // fsdp
    ex = Exchange(fsdp, rows)
    y = ex.y
    half = output_weight.shape[0]
    total = images * 2 * slot_count
    core = ex.core

    def take(array, start):
        return lax.dynamic_slice_in_dim(array, start, images, 0)

    def rows_back(own, back):
        back = back.astype(own.dtype)
        first = y == 0
        return jnp.concatenate([jnp.where(first, own, back), jnp.where(first, back, own)], axis=0)

    points = take(split_points, y * images)
    own_bound = jnp.where(y == 0, points, SEQ - points)
    bounds = jnp.stack([own_bound, SEQ - own_bound], axis=1)
    live_images = y * images + jnp.arange(images) < image_counts[0]
    bounds = jnp.concatenate([bounds, jnp.where(live_images[:, None], bounds, 0)], axis=1)

    vectors = [
        attend_gain,
        attend_shift,
        output_bias,
        dense_gain,
        dense_shift,
        down_bias,
        query_value_bias.reshape(-1),
        up_bias,
    ]
    small = [
        sum(
            jnp.pad(vectors[i][None], ((at, rows - 1 - at), (0, 128 - vectors[i].shape[0])))
            for at, i in enumerate(group)
        )
        for group in small_groups(rows)
    ]
    attend_shard = jnp.concatenate(
        [qkv_weight.reshape(rows, 3 * half), output_weight.T, *small], axis=1
    )

    xy, yx = ("x", "y"), ("y", "x")
    piece = up_weight.shape[1] // 2
    hidden = fsdp * up_bias.shape[0] * 2
    tile = math.gcd(2 * piece, 512)
    attend_blocks = ex.start_far(attend_shard)
    leaving = take_rows((1 - y).reshape(1), (tokens, cotangent))
    arriving = [ex.swap(array, "y") for array in leaving]
    pieces, arrived, _ = ex.end_far(attend_blocks, 2 * half, arriving)
    token_rows, grad_rows = (
        (take(array, y * images), other) for array, other in zip((tokens, cotangent), arrived)
    )
    pairs = ex.start(pieces, xy)
    one, two, up_shard, _ = ex.end(pairs, xy, (up_weight,))
    up_blocks = ex.start_far(up_shard)
    pairs = ex.start((one, two), yx)
    up_pieces, _, mark = ex.end_far(up_blocks, piece)
    one, two, mark = ex.end(pairs, yx, (), (mark,))
    one, two = ex.both_cores(one), ex.both_cores(two)

    attend_args = (core, bounds, *token_rows, one, two, fsdp, 2, hidden)
    pairs = ex.start(up_pieces, xy)
    *before, up_add, vec, done = attend_forward(0, *attend_args, None, (mark,))
    up_a, up_b, down_shard, mark = ex.end(pairs, xy, (down_weight.T,), (done,))
    pairs = ex.start((up_a, up_b), yx)
    down_blocks = ex.start_far(down_shard)
    first_rows, joint, chances, mixed, middle, second, done = attend_forward(
        1, *attend_args, before, (mark,)
    )
    middle = middle.reshape(total, width)
    second = second.reshape(total, width)
    down_pieces, _, mark = ex.end_far(down_blocks, piece, (), (done,))
    up_a, up_b, mark = ex.end(pairs, yx, (), (done, mark))
    up_a, up_b = ex.both_cores(up_a), ex.both_cores(up_b)

    dense_args = (core, bounds, second, *grad_rows)
    pairs = ex.start(down_pieces, xy)
    active_a, slope_a, down_a_kept, down_a_sent, done = dense_up(
        *dense_args, up_a, up_add[:1], tile, (mark,)
    )
    down_a, down_b, mark = ex.end(pairs, xy, (), (done,))
    pairs = ex.start((down_a, down_b), yx)
    active_b, slope_b, down_b_kept, down_b_sent, done = dense_up(
        *dense_args, up_b, up_add[1:], tile, (mark,)
    )
    down_a, down_b, _ = ex.end(pairs, yx, (), (done,))
    down_a, down_b = ex.both_cores(down_a), ex.both_cores(down_b)

    down_pairs = [
        ex.start_cores(down_a_kept, down_a_sent), ex.start_cores(down_b_kept, down_b_sent)
    ]
    up_a_kept, up_a_sent, up_a_sums, out_part, back_part, done = dense_down(
        core, bounds, *grad_rows, second, active_a, slope_a, up_a, down_a, tile, None, ()
    )
    kept, sent, mark = ex.add(down_pairs, yx, (done,))
    down_pairs = ex.send(kept, sent, yx)
    (
        up_b_kept,
        up_b_sent,
        up_b_sums,
        out_own,
        out_other,
        grad_middle,
        dense_sums,
        done,
    ) = dense_down(
        core,
        bounds,
        *grad_rows,
        second,
        active_b,
        slope_b,
        up_b,
        down_b,
        tile,
        (middle, vec, out_part, back_part),
        (mark,),
    )
    kept, sent, mark = ex.add(down_pairs, xy, (done,))
    down_pairs = ex.send(kept, sent, xy)
    up_pairs = [ex.start_cores(up_a_kept, up_a_sent), ex.start_cores(up_b_kept, up_b_sent)]

    back_args = (core, *token_rows, grad_middle, joint, chances, one, two, vec)
    *before, done = attend_backward(0, *back_args, [], (mark,))
    down_blocks, _, mark = ex.add_far(down_pairs, (), (done,))
    down_blocks = ex.send_far(down_blocks)
    kept, sent, mark = ex.add(up_pairs, yx, (mark,))
    up_pairs = ex.send(kept, sent, yx)
    grad_joint, grad_own, grad_other, attend_sums, done = attend_backward(
        1, *back_args, before, (mark,)
    )
    down_grad, mark = ex.sum_far(down_blocks, (done,))
    kept, sent, mark = ex.add(up_pairs, xy, (mark,))
    up_pairs = ex.send(kept, sent, xy)
    up_sums = jnp.concatenate([up_a_sums, up_b_sums], axis=0)
    one_kept, one_sent, two_kept, two_sent, done = attend_weights(
        fsdp,
        core,
        grad_middle,
        first_rows.reshape(total, width),
        mixed.reshape(total, width),
        grad_joint.reshape(total, 3 * width),
        attend_sums,
        dense_sums,
        up_sums,
        one,
        two,
        (mark,),
    )

    pairs = [ex.start_cores(one_kept, one_sent), ex.start_cores(two_kept, two_sent)]
    out_back = ex.swap(out_other, "y")
    up_blocks, (out_back,), mark = ex.add_far(up_pairs, (out_back,), (done,), 12)
    up_blocks = ex.send_far(up_blocks)
    kept, sent, mark = ex.add(pairs, yx, (mark,))
    pairs = ex.send(kept, sent, yx)
    up_grad, mark = ex.sum_far(up_blocks, (mark,))
    kept, sent, mark = ex.add(pairs, xy, (mark,))
    pairs = ex.send(kept, sent, xy)
    attend_blocks, (grad_other,), _ = ex.add_far(pairs, (grad_other,))
    attend_blocks = ex.send_far(attend_blocks)
    out_tokens = rows_back(out_own, out_back)
    grad_tokens = rows_back(grad_own, ex.swap(grad_other, "y"))
    attend_grads, _ = ex.sum_far(attend_blocks, (mark, grad_tokens))
    small_home = jnp.concatenate(
        [
            attend_grads[: len(group), 4 * half + block * 128 : 4 * half + (block + 1) * 128]
            for block, group in enumerate(small_groups(rows))
        ],
        axis=0,
    )
    grad_qkv = attend_grads[:, : 3 * half].reshape(rows, 3, half)
    grad_output = attend_grads[:, 3 * half : 4 * half].T
    plain_home = small_home[:6, :rows]
    return (
        out_tokens,
        grad_tokens,
        plain_home[0],
        plain_home[1],
        grad_qkv,
        small_home[6, :rows].reshape(2, rows // 2),
        grad_output,
        plain_home[2],
        plain_home[3],
        plain_home[4],
        up_grad,
        small_home[7, : 2 * rows],
        down_grad.T,
        plain_home[5],
    )


def solution(mesh):
    return jax.shard_map(
        partial(on_device, mesh.shape["fsdp"]),
        mesh=mesh,
        in_specs=(
            P("fsdp", "tp", None),
            P("fsdp", "tp", None),
            P("fsdp"),
            P("fsdp"),
            P("fsdp"),
            P("fsdp"),
            P("fsdp", None, "tp"),
            P(None, ("tp", "fsdp")),
            P("tp", "fsdp"),
            P("fsdp"),
            P("fsdp"),
            P("fsdp"),
            P("fsdp", "tp"),
            P(("tp", "fsdp")),
            P("tp", "fsdp"),
            P("fsdp"),
        ),
        out_specs=(
            P("fsdp", "tp", None),
            P("fsdp", "tp", None),
            P("fsdp"),
            P("fsdp"),
            P("fsdp", None, "tp"),
            P(None, ("tp", "fsdp")),
            P("tp", "fsdp"),
            P("fsdp"),
            P("fsdp"),
            P("fsdp"),
            P("fsdp", "tp"),
            P(("tp", "fsdp")),
            P("tp", "fsdp"),
            P("fsdp"),
        ),
        check_vma=False,
    )
```

profile of v0, /device:TPU:0, one launch (start us, length us, event | category | flops | bytes accessed | tf_op | source)
XLA Modules:
  0.0 263.8 jit_solution(9343540089855867215)
XLA Ops:
  3.1 3.0 %collective-permute-start.3 = (bf16[2,128,768]{2,1,0:T(8,128)(2,1)S(1)}, bf16[2,128,768]{2,1,0:T(8,128)(2,1)S(1)}, u32[]{:S(2)}, u32[]{:S(2)}) collective-permute-start(bf16[2,128,768]{2,1,0:T(8,128)(2,1)S(1)} %get-tuple-element.150), channel_id=1, source_target_pairs={{0,1},{1,0},{2,3},{3,2},{4,5},{5,4},{6,7},{7,6},{8,9},{9,8},{10,11... | collective-permute-start | bytes 1179656 | tf_op jit(solution)/shard_map/ppermute | solution.py:921
  6.5 2.1 collective-permute-start
  8.5 2.6 collective-permute-start.1
  11.2 2.8 %collective-permute-done.refs_2_ = bf16[1,48,1664]{2,1,0:T(8,128)(2,1)S(1)} collective-permute-done((bf16[1,48,1664]{2,1,0:T(8,128)(2,1)S(1)}, bf16[1,48,1664]{2,1,0:T(8,128)(2,1)S(1)}, u32[]{:S(2)}, u32[]{:S(2)}) %collective-permute-start) | collective-permute-done | bytes 159776 | tf_op jit(solution)/shard_map/ppermute | solution.py:923
  14.0 9.0 %collective-permute-done.1.refs_3_ = bf16[1,48,1664]{2,1,0:T(8,128)(2,1)S(1)} collective-permute-done((bf16[1,48,1664]{2,1,0:T(8,128)(2,1)S(1)}, bf16[1,48,1664]{2,1,0:T(8,128)(2,1)S(1)}, u32[]{:S(2)}, u32[]{:S(2)}) %collective-permute-start.1) | collective-permute-done | bytes 159776 | tf_op jit(solution)/shard_map/ppermute | solution.py:923
  28.1 6.1 %collective-permute-done.5.refs_2_ = bf16[4,48,768]{2,1,0:T(8,128)(2,1)S(1)} collective-permute-done((bf16[4,48,768]{2,1,0:T(8,128)(2,1)S(1)}, bf16[4,48,768]{2,1,0:T(8,128)(2,1)S(1)}, u32[]{:S(2)}, u32[]{:S(2)}) %collective-permute-start.5) | collective-permute-done | bytes 294944 | tf_op jit(solution)/shard_map/ppermute | solution.py:923
  38.1 2.6 collective-permute-start.10
  42.3 7.9 %collective-permute-done.10.refs_3_ = bf16[1,48,1536]{2,1,0:T(8,128)(2,1)S(1)} collective-permute-done((bf16[1,48,1536]{2,1,0:T(8,128)(2,1)S(1)}, bf16[1,48,1536]{2,1,0:T(8,128)(2,1)S(1)}, u32[]{:S(2)}, u32[]{:S(2)}) %collective-permute-start.10) | collective-permute-done | bytes 147488 | tf_op jit(solution)/shard_map/ppermute | solution.py:923
  51.3 2.5 join_pieces.7
  59.0 9.6 %attend_forward.2 = (bf16[2,256,768]{2,1,0:T(8,128)(2,1)}, bf16[2,256,2304]{2,1,0:T(8,128)(2,1)}, bf16[2,6,512,256]{3,2,1,0:T(8,128)(2,1)}, bf16[2,256,768]{2,1,...) custom-call(s32[1]{0:T(128)} %bitcast.refs_0_, ...), custom_call_target="tpu_custom_call" | custom-call | flops 8999999488 | bytes 100000 | tf_op jit(solution)/shard_map/attend_forward/pallas_call | solution.py:537
  70.3 2.4 collective-permute-start.18
  77.2 8.1 %attend_forward.3 = (bf16[2,256,768]{2,1,0:T(8,128)(2,1)}, bf16[2,256,2304]{2,1,0:T(8,128)(2,1)}, bf16[2,6,512,256]{3,2,1,0:T(8,128)(2,1)}, bf16[2,256,768]{2,1,...) custom-call(s32[1]{0:T(128)} %bitcast.refs_0_, ...), custom_call_target="tpu_custom_call", output_to_operand_aliasing={{0}: (8, {}), {1}: (9, {}), {2}: (10, {}), {3}: (11, {}), {... | custom-call | flops 8999999488 | bytes 100000 | tf_op jit(solution)/shard_map/attend_forward/pallas_call | solution.py:537
  88.3 2.6 collective-permute-done.16.refs_2_
  91.2 2.5 join_pieces.9
  96.5 7.4 %dense_up.2 = (bf16[512,1536]{1,0:T(8,128)(2,1)}, bf16[512,1536]{1,0:T(8,128)(2,1)}, bf16[8,48,1536]{2,1,0:T(8,128)(2,1)S(1)}, bf16[8,48,1536]{2,1,0:T(8,128)(2,1)S(1)}, s32[1]{0:T(128)}) custom-call(s32[1]{0:T(128)} %bitcast.refs_0_, s32[2,4]{1,0:T(2,128)S(1)} %pad_add_fusion.1.refs_1_, bf16[512,768]{1,0:T(8,128)(2,1)S(1)} %bitcast.160, ...), custom_call_target="tpu_custom_call" | custom-call | flops 8000000000 | bytes 100000 | tf_op jit(solution)/shard_map/dense_up/pallas_call | solution.py:573
  108.3 7.7 %dense_up.3 = (bf16[512,1536]{1,0:T(8,128)(2,1)}, bf16[512,1536]{1,0:T(8,128)(2,1)}, bf16[8,48,1536]{2,1,0:T(8,128)(2,1)S(1)}, bf16[8,48,1536]{2,1,0:T(8,128)(2,1)S(1)}, s32[1]{0:T(128)}) custom-call(s32[1]{0:T(128)} %bitcast.refs_0_, s32[2,4]{1,0:T(2,128)S(1)} %pad_add_fusion.1.refs_1_, bf16[512,768]{1,0:T(8,128)(2,1)S(1)} %bitcast.161, ...), custom_call_target="tpu_custom_call" | custom-call | flops 8000000000 | bytes 100000 | tf_op jit(solution)/shard_map/dense_up/pallas_call | solution.py:573
  116.0 5.1 %collective-permute-done.25.refs_2_ = bf16[8,48,768]{2,1,0:T(8,128)(2,1)S(1)} collective-permute-done((bf16[8,48,768]{2,1,0:T(8,128)(2,1)S(1)}, bf16[8,48,768]{2,1,0:T(8,128)(2,1)S(1)}, u32[]{:S(2)}, u32[]{:S(2)}) %collective-permute-start.25) | collective-permute-done | bytes 589856 | tf_op jit(solution)/shard_map/ppermute | solution.py:921
  127.0 10.3 %dense_down.2 = (bf16[8,48,1536]{2,1,0:T(8,128)(2,1)S(1)}, bf16[8,48,1536]{2,1,0:T(8,128)(2,1)S(1)}, f32[1,1536]{1,0:T(1,128)S(1)}, f32[512,768]{1,0:T(8,128)}, f32[512,768]{1,0:T(8,128)}, /*index=5*/s32[1]{0:T(128)}) custom-call(s32[1]{0:T(128)} %bitcast.refs_0_, s32[2,4]{1,0:T(2,128)S(1)} %pad_add_fusion.1.refs_1_, ...), custom_call_target="tpu_custom_call" | custom-call | flops 12000000000 | bytes 100000 | tf_op jit(solution)/shard_map/dense_down/pallas_call | solution.py:615
  143.4 12.3 %dense_down.3 = (bf16[8,48,1536]{2,1,0:T(8,128)(2,1)S(1)}, bf16[8,48,1536]{2,1,0:T(8,128)(2,1)S(1)}, f32[1,1536]{1,0:T(1,128)S(1)}, bf16[2,128,768]{2,1,0:T(8,12...) custom-call(s32[1]{0:T(128)} %bitcast.refs_0_, ...), custom_call_target="tpu_custom_call" | custom-call | flops 12000000000 | bytes 100000 | tf_op jit(solution)/shard_map/dense_down/pallas_call | solution.py:615
  162.5 8.1 %attend_backward.2 = (bf16[2,256,2304]{2,1,0:T(8,128)(2,1)}, f32[2,128,768]{2,1,0:T(8,128)S(1)}, bf16[2,128,768]{2,1,0:T(8,128)(2,1)S(1)}, f32[2,8,768]{2,1,0:T(8,128)S(1)}, s32[1]{0:T(128)}) custom-call(s32[1]{0:T(128)} %bitcast.refs_0_, bf16[2,128,768]{2,1,0:T(8,128)(2,1)S(1)} %constant_dynamic-slice_fusion.refs_2_.refs_1_, ...), custom_call_target="tpu_custom_call" | custom-call | flops 10000000000 | bytes 100000 | tf_op jit(solution)/shard_map/attend_backward/pallas_call | solution.py:679
  172.9 2.4 collective-permute-start.40
  179.8 8.9 %attend_backward.3 = (bf16[2,256,2304]{2,1,0:T(8,128)(2,1)}, f32[2,128,768]{2,1,0:T(8,128)S(1)}, bf16[2,128,768]{2,1,0:T(8,128)(2,1)S(1)}, f32[2,8,768]{2,1,0:T(8,128)S(1)}, s32[1]{0:T(128)}) custom-call(s32[1]{0:T(128)} %bitcast.refs_0_, ...), custom_call_target="tpu_custom_call", output_to_operand_aliasing={{0}: (11, {}), {1}: (12, {}), {2}: (13, {}), {3}: (14, {})} | custom-call | flops 10000000000 | bytes 100000 | tf_op jit(solution)/shard_map/attend_backward/pallas_call | solution.py:679
  191.6 3.2 %collective-permute-done.37 = bf16[8,48,768]{2,1,0:T(8,128)(2,1)S(1)} collective-permute-done((bf16[8,48,768]{2,1,0:T(8,128)(2,1)S(1)}, bf16[8,48,768]{2,1,0:T(8,128)(2,1)S(1)}, u32[]{:S(2)}, u32[]{:S(2)}) %collective-permute-start.37) | collective-permute-done | bytes 589856 | tf_op jit(solution)/shard_map/ppermute | solution.py:921
  197.2 8.1 %attend_weights.1 = (bf16[8,48,1536]{2,1,0:T(8,128)(2,1)S(1)}, bf16[8,48,1536]{2,1,0:T(8,128)(2,1)S(1)}, bf16[8,48,1792]{2,1,0:T(8,128)(2,1)S(1)}, bf16[8,48,1792]{2,1,0:T(8,128)(2,1)S(1)}, s32[1]{0:T(128)}) custom-call(s32[1]{0:T(128)} %bitcast.refs_0_, f32[512,768]{1,0:T(8,128)S(1)} %copy-done.15, bf16[512,768]{1,0:T(8,128)(2,1)S(1)} %bitcast.158, ...), custom_call_target="tpu_custom_call" | custom-call | flops 6000000000 | bytes 100000 | tf_op jit(solution)/shard_map/attend_weights/pallas_call | solution.py:712
  211.9 2.0 collective-permute-start.48
  215.7 2.9 %collective-permute-start.50 = (bf16[1,48,1536]{2,1,0:T(8,128)(2,1)S(1)}, bf16[1,48,1536]{2,1,0:T(8,128)(2,1)S(1)}, u32[]{:S(2)}, u32[]{:S(2)}) collective-permute-start(bf16[1,48,1536]{2,1,0:T(8,128)(2,1)S(1)} %get-tuple-element.268), channel_id=1, source_target_pairs={{0,16},{2,18},{4,20},{6,22},{8,24},{10,26},{12,28},{14,30},{16,0},... | collective-permute-start | bytes 442376 | tf_op jit(solution)/shard_map/ppermute | solution.py:923
  220.1 3.3 %collective-permute-done.49.refs_1_ = bf16[1,48,1536]{2,1,0:T(8,128)(2,1)S(1)} collective-permute-done((bf16[1,48,1536]{2,1,0:T(8,128)(2,1)S(1)}, bf16[1,48,1536]{2,1,0:T(8,128)(2,1)S(1)}, u32[]{:S(2)}, u32[]{:S(2)}) %collective-permute-start.49) | collective-permute-done | bytes 147488 | tf_op jit(solution)/shard_map/ppermute | solution.py:923
  223.3 6.3 %collective-permute-done.50.refs_2_ = bf16[1,48,1536]{2,1,0:T(8,128)(2,1)S(1)} collective-permute-done((bf16[1,48,1536]{2,1,0:T(8,128)(2,1)S(1)}, bf16[1,48,1536]{2,1,0:T(8,128)(2,1)S(1)}, u32[]{:S(2)}, u32[]{:S(2)}) %collective-permute-start.50) | collective-permute-done | bytes 147488 | tf_op jit(solution)/shard_map/ppermute | solution.py:923
  235.0 6.2 %collective-permute-done.52 = bf16[4,48,768]{2,1,0:T(8,128)(2,1)S(1)} collective-permute-done((bf16[4,48,768]{2,1,0:T(8,128)(2,1)S(1)}, bf16[4,48,768]{2,1,0:T(8,128)(2,1)S(1)}, u32[]{:S(2)}, u32[]{:S(2)}) %collective-permute-start.52) | collective-permute-done | bytes 294944 | tf_op jit(solution)/shard_map/ppermute | solution.py:923
  244.7 2.1 collective-permute-start.55
  249.3 2.1 collective-permute-done.54
  251.6 7.6 %collective-permute-done.56.refs_2_ = bf16[1,48,1664]{2,1,0:T(8,128)(2,1)S(1)} collective-permute-done((bf16[1,48,1664]{2,1,0:T(8,128)(2,1)S(1)}, bf16[1,48,1664]{2,1,0:T(8,128)(2,1)S(1)}, u32[]{:S(2)}, u32[]{:S(2)}) %collective-permute-start.56) | collective-permute-done | bytes 159776 | tf_op jit(solution)/shard_map/ppermute | solution.py:923
  (210 shorter events, 91.7 us)
Async XLA Ops:
  3.1 19.9 %collective-permute-start.3 = (bf16[2,128,768]{2,1,0:T(8,128)(2,1)S(1)}, bf16[2,128,768]{2,1,0:T(8,128)(2,1)S(1)}, u32[]{:S(2)}, u32[]{:S(2)}) collective-permute-start(bf16[2,128,768]{2,1,0:T(8,128)(2,1)S(1)} %get-tuple-element.150), channel_id=1, source_target_pairs={{0,1},{1,0},{2,3},{3,2},{4,5},{5,4},{6,7},{7,6},{8,9},{9,8},{10,11... | collective-permute-start | bytes 1179656 | tf_op jit(solution)/shard_map/ppermute | solution.py:921
  6.1 17.5 %collective-permute-start.4 = (bf16[2,128,768]{2,1,0:T(8,128)(2,1)S(1)}, bf16[2,128,768]{2,1,0:T(8,128)(2,1)S(1)}, u32[]{:S(2)}, u32[]{:S(2)}) collective-permute-start(bf16[2,128,768]{2,1,0:T(8,128)(2,1)S(1)} %get-tuple-element.151), channel_id=1, source_target_pairs={{0,1},{1,0},{2,3},{3,2},{4,5},{5,4},{6,7},{7,6},{8,9},{9,8},{10,11... | collective-permute-start | bytes 1179656 | tf_op jit(solution)/shard_map/ppermute | solution.py:921
  8.5 14.5 %collective-permute-start.1 = (bf16[1,48,1664]{2,1,0:T(8,128)(2,1)S(1)}, bf16[1,48,1664]{2,1,0:T(8,128)(2,1)S(1)}, u32[]{:S(2)}, u32[]{:S(2)}) collective-permute-start(bf16[1,48,1664]{2,1,0:T(8,128)(2,1)S(1)} %maximum_bitcast_fusion.refs_1_), channel_id=1, source_target_pairs={{0,16},{2,18},{4,20},{6,22},{8,24},{10,26},{12,28},{14,30},{16,0},... | collective-permute-start | bytes 479240 | tf_op jit(solution)/shard_map/ppermute | solution.py:923
  35.2 16.0 %collective-permute-start.8 = (bf16[4,48,1792]{2,1,0:T(8,128)(2,1)S(1)}, bf16[4,48,1792]{2,1,0:T(8,128)(2,1)S(1)}, u32[]{:S(2)}, u32[]{:S(2)}) collective-permute-start(bf16[4,48,1792]{2,1,0:T(8,128)(2,1)S(1)} %get-tuple-element.157.refs_3_), channel_id=1, source_target_pairs={{0,4},{2,6},{4,0},{6,2},{8,12},{10,14},{12,8},{14,10},{16,20},{18,... | collective-permute-start | bytes 2064392 | tf_op jit(solution)/shard_map/ppermute | solution.py:923
  36.8 14.4 %collective-permute-start.7 = (bf16[8,48,768]{2,1,0:T(8,128)(2,1)S(1)}, bf16[8,48,768]{2,1,0:T(8,128)(2,1)S(1)}, u32[]{:S(2)}, u32[]{:S(2)}) collective-permute-start(bf16[8,48,768]{2,1,0:T(8,128)(2,1)S(1)} %bitcast.104), channel_id=1, source_target_pairs={{0,1},{1,0},{2,3},{3,2},{4,5},{5,4},{6,7},{7,6},{8,9},{9,8},{10,11... | collective-permute-start | bytes 1769480 | tf_op jit(solution)/shard_map/ppermute | solution.py:921
  55.5 13.1 %collective-permute-start.14 = (bf16[4,48,768]{2,1,0:T(8,128)(2,1)S(1)}, bf16[4,48,768]{2,1,0:T(8,128)(2,1)S(1)}, u32[]{:S(2)}, u32[]{:S(2)}) collective-permute-start(bf16[4,48,768]{2,1,0:T(8,128)(2,1)S(1)} %bitcast.113), channel_id=1, source_target_pairs={{0,4},{2,6},{4,0},{6,2},{8,12},{10,14},{12,8},{14,10},{16,20},{18,... | collective-permute-start | bytes 884744 | tf_op jit(solution)/shard_map/ppermute | solution.py:923
  56.2 12.4 %collective-permute-start.15 = (bf16[4,48,768]{2,1,0:T(8,128)(2,1)S(1)}, bf16[4,48,768]{2,1,0:T(8,128)(2,1)S(1)}, u32[]{:S(2)}, u32[]{:S(2)}) collective-permute-start(bf16[4,48,768]{2,1,0:T(8,128)(2,1)S(1)} %bitcast.115), channel_id=1, source_target_pairs={{0,1},{1,0},{2,3},{3,2},{4,5},{5,4},{6,7},{7,6},{8,9},{9,8},{10,11... | collective-permute-start | bytes 884744 | tf_op jit(solution)/shard_map/ppermute | solution.py:921
  70.3 15.0 %collective-permute-start.18 = (bf16[1,48,1536]{2,1,0:T(8,128)(2,1)S(1)}, bf16[1,48,1536]{2,1,0:T(8,128)(2,1)S(1)}, u32[]{:S(2)}, u32[]{:S(2)}) collective-permute-start(bf16[1,48,1536]{2,1,0:T(8,128)(2,1)S(1)} %bitcast.134), channel_id=1, source_target_pairs={{0,8},{2,10},{4,12},{6,14},{8,0},{10,2},{12,4},{14,6},{16,24},{18,... | collective-permute-start | bytes 442376 | tf_op jit(solution)/shard_map/ppermute | solution.py:923
  72.7 13.9 %collective-permute-start.19 = (bf16[1,48,1536]{2,1,0:T(8,128)(2,1)S(1)}, bf16[1,48,1536]{2,1,0:T(8,128)(2,1)S(1)}, u32[]{:S(2)}, u32[]{:S(2)}) collective-permute-start(bf16[1,48,1536]{2,1,0:T(8,128)(2,1)S(1)} %bitcast.135), channel_id=1, source_target_pairs={{0,16},{2,18},{4,20},{6,22},{8,24},{10,26},{12,28},{14,30},{16,0},... | collective-permute-start | bytes 442376 | tf_op jit(solution)/shard_map/ppermute | solution.py:923
  76.1 14.8 %collective-permute-start.16 = (bf16[8,48,768]{2,1,0:T(8,128)(2,1)S(1)}, bf16[8,48,768]{2,1,0:T(8,128)(2,1)S(1)}, u32[]{:S(2)}, u32[]{:S(2)}) collective-permute-start(bf16[8,48,768]{2,1,0:T(8,128)(2,1)S(1)} %bitcast.98), channel_id=1, source_target_pairs={{0,1},{1,0},{2,3},{3,2},{4,5},{5,4},{6,7},{7,6},{8,9},{9,8},{10,11... | collective-permute-start | bytes 1769480 | tf_op jit(solution)/shard_map/ppermute | solution.py:921
  76.6 14.5 %collective-permute-start.17 = (bf16[4,48,1536]{2,1,0:T(8,128)(2,1)S(1)}, bf16[4,48,1536]{2,1,0:T(8,128)(2,1)S(1)}, u32[]{:S(2)}, u32[]{:S(2)}) collective-permute-start(bf16[4,48,1536]{2,1,0:T(8,128)(2,1)S(1)} %get-tuple-element.175.refs_3_), channel_id=1, source_target_pairs={{0,4},{2,6},{4,0},{6,2},{8,12},{10,14},{12,8},{14,10},{16,20},{18,... | collective-permute-start | bytes 1769480 | tf_op jit(solution)/shard_map/ppermute | solution.py:923
  93.8 14.6 %collective-permute-start.21 = (bf16[8,48,1536]{2,1,0:T(8,128)(2,1)S(1)}, bf16[8,48,1536]{2,1,0:T(8,128)(2,1)S(1)}, u32[]{:S(2)}, u32[]{:S(2)}) collective-permute-start(bf16[8,48,1536]{2,1,0:T(8,128)(2,1)S(1)} %bitcast.147), channel_id=1, source_target_pairs={{0,2},{2,0},{4,6},{6,4},{8,10},{10,8},{12,14},{14,12},{16,18},{18,... | collective-permute-start | bytes 3538952 | tf_op jit(solution)/shard_map/ppermute | solution.py:923
  105.6 15.4 %collective-permute-start.25 = (bf16[8,48,768]{2,1,0:T(8,128)(2,1)S(1)}, bf16[8,48,768]{2,1,0:T(8,128)(2,1)S(1)}, u32[]{:S(2)}, u32[]{:S(2)}) collective-permute-start(bf16[8,48,768]{2,1,0:T(8,128)(2,1)S(1)} %bitcast.107), channel_id=1, source_target_pairs={{0,1},{1,0},{2,3},{3,2},{4,5},{5,4},{6,7},{7,6},{8,9},{9,8},{10,11... | collective-permute-start | bytes 1769480 | tf_op jit(solution)/shard_map/ppermute | solution.py:921
  107.2 15.1 %collective-permute-start.26 = (bf16[4,48,1536]{2,1,0:T(8,128)(2,1)S(1)}, bf16[4,48,1536]{2,1,0:T(8,128)(2,1)S(1)}, u32[]{:S(2)}, u32[]{:S(2)}) collective-permute-start(bf16[4,48,1536]{2,1,0:T(8,128)(2,1)S(1)} %get-tuple-element.190.refs_3_), channel_id=1, source_target_pairs={{0,4},{2,6},{4,0},{6,2},{8,12},{10,14},{12,8},{14,10},{16,20},{18,... | collective-permute-start | bytes 1769480 | tf_op jit(solution)/shard_map/ppermute | solution.py:923
  124.2 13.2 %collective-permute-start.30 = (bf16[8,48,1536]{2,1,0:T(8,128)(2,1)S(1)}, bf16[8,48,1536]{2,1,0:T(8,128)(2,1)S(1)}, u32[]{:S(2)}, u32[]{:S(2)}) collective-permute-start(bf16[8,48,1536]{2,1,0:T(8,128)(2,1)S(1)} %get-tuple-element.203), channel_id=1, source_target_pairs={{0,2},{2,0},{4,6},{6,4},{8,10},{10,8},{12,14},{14,12},{16,18},{18,... | collective-permute-start | bytes 3538952 | tf_op jit(solution)/shard_map/ppermute | solution.py:923
  124.7 12.7 %collective-permute-start.29 = (bf16[8,48,1536]{2,1,0:T(8,128)(2,1)S(1)}, bf16[8,48,1536]{2,1,0:T(8,128)(2,1)S(1)}, u32[]{:S(2)}, u32[]{:S(2)}) collective-permute-start(bf16[8,48,1536]{2,1,0:T(8,128)(2,1)S(1)} %get-tuple-element.201), channel_id=1, source_target_pairs={{0,2},{2,0},{4,6},{6,4},{8,10},{10,8},{12,14},{14,12},{16,18},{18,... | collective-permute-start | bytes 3538952 | tf_op jit(solution)/shard_map/ppermute | solution.py:923
  124.7 15.8 %collective-permute-start.27 = (bf16[8,48,1536]{2,1,0:T(8,128)(2,1)S(1)}, bf16[8,48,1536]{2,1,0:T(8,128)(2,1)S(1)}, u32[]{:S(2)}, u32[]{:S(2)}) collective-permute-start(bf16[8,48,1536]{2,1,0:T(8,128)(2,1)S(1)} %bitcast.150), channel_id=1, source_target_pairs={{0,2},{2,0},{4,6},{6,4},{8,10},{10,8},{12,14},{14,12},{16,18},{18,... | collective-permute-start | bytes 3538952 | tf_op jit(solution)/shard_map/ppermute | solution.py:923
  139.3 17.0 %collective-permute-start.33 = (bf16[8,48,768]{2,1,0:T(8,128)(2,1)S(1)}, bf16[8,48,768]{2,1,0:T(8,128)(2,1)S(1)}, u32[]{:S(2)}, u32[]{:S(2)}) collective-permute-start(bf16[8,48,768]{2,1,0:T(8,128)(2,1)S(1)} %get-tuple-element.212), channel_id=1, source_target_pairs={{0,1},{1,0},{2,3},{3,2},{4,5},{5,4},{6,7},{7,6},{8,9},{9,8},{10,11... | collective-permute-start | bytes 1769480 | tf_op jit(solution)/shard_map/ppermute | solution.py:921
  139.9 16.4 %collective-permute-start.34 = (bf16[4,48,1536]{2,1,0:T(8,128)(2,1)S(1)}, bf16[4,48,1536]{2,1,0:T(8,128)(2,1)S(1)}, u32[]{:S(2)}, u32[]{:S(2)}) collective-permute-start(bf16[4,48,1536]{2,1,0:T(8,128)(2,1)S(1)} %get-tuple-element.214), channel_id=1, source_target_pairs={{0,4},{2,6},{4,0},{6,2},{8,12},{10,14},{12,8},{14,10},{16,20},{18,... | collective-permute-start | bytes 1769480 | tf_op jit(solution)/shard_map/ppermute | solution.py:923
  155.7 21.1 %collective-permute-start.32 = (bf16[8,48,1536]{2,1,0:T(8,128)(2,1)S(1)}, bf16[8,48,1536]{2,1,0:T(8,128)(2,1)S(1)}, u32[]{:S(2)}, u32[]{:S(2)}) collective-permute-start(bf16[8,48,1536]{2,1,0:T(8,128)(2,1)S(1)} %get-tuple-element.210), channel_id=1, source_target_pairs={{0,2},{2,0},{4,6},{6,4},{8,10},{10,8},{12,14},{14,12},{16,18},{18,... | collective-permute-start | bytes 3538952 | tf_op jit(solution)/shard_map/ppermute | solution.py:923
  155.8 21.0 %collective-permute-start.31 = (bf16[8,48,1536]{2,1,0:T(8,128)(2,1)S(1)}, bf16[8,48,1536]{2,1,0:T(8,128)(2,1)S(1)}, u32[]{:S(2)}, u32[]{:S(2)}) collective-permute-start(bf16[8,48,1536]{2,1,0:T(8,128)(2,1)S(1)} %get-tuple-element.208), channel_id=1, source_target_pairs={{0,2},{2,0},{4,6},{6,4},{8,10},{10,8},{12,14},{14,12},{16,18},{18,... | collective-permute-start | bytes 3538952 | tf_op jit(solution)/shard_map/ppermute | solution.py:923
  158.2 12.4 %collective-permute-start.35 = (bf16[4,48,768]{2,1,0:T(8,128)(2,1)S(1)}, bf16[4,48,768]{2,1,0:T(8,128)(2,1)S(1)}, u32[]{:S(2)}, u32[]{:S(2)}) collective-permute-start(bf16[4,48,768]{2,1,0:T(8,128)(2,1)S(1)} %get-tuple-element.217), channel_id=1, source_target_pairs={{0,4},{2,6},{4,0},{6,2},{8,12},{10,14},{12,8},{14,10},{16,20},{18,... | collective-permute-start | bytes 884744 | tf_op jit(solution)/shard_map/ppermute | solution.py:923
  172.3 16.4 %collective-permute-start.39 = (bf16[1,48,1536]{2,1,0:T(8,128)(2,1)S(1)}, bf16[1,48,1536]{2,1,0:T(8,128)(2,1)S(1)}, u32[]{:S(2)}, u32[]{:S(2)}) collective-permute-start(bf16[1,48,1536]{2,1,0:T(8,128)(2,1)S(1)} %get-tuple-element.231), channel_id=1, source_target_pairs={{0,8},{2,10},{4,12},{6,14},{8,0},{10,2},{12,4},{14,6},{16,24},{18,... | collective-permute-start | bytes 442376 | tf_op jit(solution)/shard_map/ppermute | solution.py:923
  172.9 17.2 %collective-permute-start.40 = (bf16[1,48,1536]{2,1,0:T(8,128)(2,1)S(1)}, bf16[1,48,1536]{2,1,0:T(8,128)(2,1)S(1)}, u32[]{:S(2)}, u32[]{:S(2)}) collective-permute-start(bf16[1,48,1536]{2,1,0:T(8,128)(2,1)S(1)} %get-tuple-element.232), channel_id=1, source_target_pairs={{0,16},{2,18},{4,20},{6,22},{8,24},{10,26},{12,28},{14,30},{16,0},... | collective-permute-start | bytes 442376 | tf_op jit(solution)/shard_map/ppermute | solution.py:923
  175.4 14.8 %collective-permute-start.41 = (bf16[1,48,1536]{2,1,0:T(8,128)(2,1)S(1)}, bf16[1,48,1536]{2,1,0:T(8,128)(2,1)S(1)}, u32[]{:S(2)}, u32[]{:S(2)}) collective-permute-start(bf16[1,48,1536]{2,1,0:T(8,128)(2,1)S(1)} %get-tuple-element.233), channel_id=1, source_target_pairs={{0,24},{2,26},{4,28},{6,30},{8,16},{10,18},{12,20},{14,22},{16,8},... | collective-permute-start | bytes 442376 | tf_op jit(solution)/shard_map/ppermute | solution.py:923
  178.5 16.3 %collective-permute-start.37 = (bf16[8,48,768]{2,1,0:T(8,128)(2,1)S(1)}, bf16[8,48,768]{2,1,0:T(8,128)(2,1)S(1)}, u32[]{:S(2)}, u32[]{:S(2)}) collective-permute-start(bf16[8,48,768]{2,1,0:T(8,128)(2,1)S(1)} %get-tuple-element.227), channel_id=1, source_target_pairs={{0,1},{1,0},{2,3},{3,2},{4,5},{5,4},{6,7},{7,6},{8,9},{9,8},{10,11... | collective-permute-start | bytes 1769480 | tf_op jit(solution)/shard_map/ppermute | solution.py:921
  179.1 15.7 %collective-permute-start.38 = (bf16[4,48,1536]{2,1,0:T(8,128)(2,1)S(1)}, bf16[4,48,1536]{2,1,0:T(8,128)(2,1)S(1)}, u32[]{:S(2)}, u32[]{:S(2)}) collective-permute-start(bf16[4,48,1536]{2,1,0:T(8,128)(2,1)S(1)} %get-tuple-element.229), channel_id=1, source_target_pairs={{0,4},{2,6},{4,0},{6,2},{8,12},{10,14},{12,8},{14,10},{16,20},{18,... | collective-permute-start | bytes 1769480 | tf_op jit(solution)/shard_map/ppermute | solution.py:923
  188.7 17.2 %collective-permute-start.44 = (bf16[2,128,768]{2,1,0:T(8,128)(2,1)S(1)}, bf16[2,128,768]{2,1,0:T(8,128)(2,1)S(1)}, u32[]{:S(2)}, u32[]{:S(2)}) collective-permute-start(bf16[2,128,768]{2,1,0:T(8,128)(2,1)S(1)} %get-tuple-element.245), channel_id=1, source_target_pairs={{0,1},{1,0},{2,3},{3,2},{4,5},{5,4},{6,7},{7,6},{8,9},{9,8},{10,11... | collective-permute-start | bytes 1179656 | tf_op jit(solution)/shard_map/ppermute | solution.py:921
  211.9 19.2 %collective-permute-start.48 = (bf16[4,48,1792]{2,1,0:T(8,128)(2,1)S(1)}, bf16[4,48,1792]{2,1,0:T(8,128)(2,1)S(1)}, u32[]{:S(2)}, u32[]{:S(2)}) collective-permute-start(bf16[4,48,1792]{2,1,0:T(8,128)(2,1)S(1)} %get-tuple-element.265), channel_id=1, source_target_pairs={{0,4},{2,6},{4,0},{6,2},{8,12},{10,14},{12,8},{14,10},{16,20},{18,... | collective-permute-start | bytes 2064392 | tf_op jit(solution)/shard_map/ppermute | solution.py:923
  213.9 17.2 %collective-permute-start.47 = (bf16[8,48,768]{2,1,0:T(8,128)(2,1)S(1)}, bf16[8,48,768]{2,1,0:T(8,128)(2,1)S(1)}, u32[]{:S(2)}, u32[]{:S(2)}) collective-permute-start(bf16[8,48,768]{2,1,0:T(8,128)(2,1)S(1)} %get-tuple-element.263), channel_id=1, source_target_pairs={{0,1},{1,0},{2,3},{3,2},{4,5},{5,4},{6,7},{7,6},{8,9},{9,8},{10,11... | collective-permute-start | bytes 1769480 | tf_op jit(solution)/shard_map/ppermute | solution.py:921
  215.7 14.0 %collective-permute-start.50 = (bf16[1,48,1536]{2,1,0:T(8,128)(2,1)S(1)}, bf16[1,48,1536]{2,1,0:T(8,128)(2,1)S(1)}, u32[]{:S(2)}, u32[]{:S(2)}) collective-permute-start(bf16[1,48,1536]{2,1,0:T(8,128)(2,1)S(1)} %get-tuple-element.268), channel_id=1, source_target_pairs={{0,16},{2,18},{4,20},{6,22},{8,24},{10,26},{12,28},{14,30},{16,0},... | collective-permute-start | bytes 442376 | tf_op jit(solution)/shard_map/ppermute | solution.py:923
  246.9 12.4 %collective-permute-start.56 = (bf16[1,48,1664]{2,1,0:T(8,128)(2,1)S(1)}, bf16[1,48,1664]{2,1,0:T(8,128)(2,1)S(1)}, u32[]{:S(2)}, u32[]{:S(2)}) collective-permute-start(bf16[1,48,1664]{2,1,0:T(8,128)(2,1)S(1)} %get-tuple-element.280), channel_id=1, source_target_pairs={{0,16},{2,18},{4,20},{6,22},{8,24},{10,26},{12,28},{14,30},{16,0},... | collective-permute-start | bytes 479240 | tf_op jit(solution)/shard_map/ppermute | solution.py:923
  (61 other events, 543.7 us)
where the time goes:
time: 267 us; the launch traced here: 264 us
  Pallas kernels  115 us (43%)
  waiting for transfers between devices  71.5 us (27%)
  starting transfers between devices  63.3 us (24%)
  local copies, waits for them, and re-layouts  10 us (4%)
    ppermute x42, waiting for transfers between devices, swap(): lax.ppermute(value, 'fsdp', [(i, i ^ apart) for i in range(self.fsdp)])  56.6 us
    ppermute x42, starting transfers between devices, swap(): lax.ppermute(value, 'fsdp', [(i, i ^ apart) for i in range(self.fsdp)])  44.2 us
    pallas_call x2, Pallas kernels, dense_down(): pl.pallas_call(ordered(partial(dense_down_kernel, opening), 11 if opening...  22.6 us
    ppermute x16, starting transfers between devices, swap(): return lax.ppermute(value, 'tp', [(0, 1), (1, 0)])  19.1 us
    pallas_call x2, Pallas kernels, attend_forward(): pl.pallas_call(ordered(partial(attend_forward_kernel, image, made, fsdp),...  17.7 us
    pallas_call x2, Pallas kernels, attend_backward(): pl.pallas_call(ordered(attend_backward_kernel, 11 + len(before), len(earl...  17 us
    pallas_call x2, Pallas kernels, dense_up(): pl.pallas_call(ordered(dense_up_kernel, 8, len(earlier), 2), grid=(column...  15 us
    ppermute x16, waiting for transfers between devices, swap(): return lax.ppermute(value, 'tp', [(0, 1), (1, 0)])  15 us
  transfers between devices with their start and end apart: 58, of which 21 were waited for; matrix products, arithmetic and copies ran while one was open for 1% of the time, Pallas kernels for 37%

commit v1 on v0

--- a/solution.py
+++ b/solution.py
@@ -257,7 +257,7 @@
     kept_ref,
     sent_ref,
     up_whole,
-    grad_in,
+    grad_turned,
 ):
     images, slot_count, _ = own_ref.shape
     length = 2 * slot_count
@@ -266,7 +266,8 @@
     def _():
         for image in range(images):
             rows = slice(image * length, (image + 1) * length)
-            grad_in[rows] = masked_grads(bounds_ref, own_ref, other_ref, image).astype(bf16)
+            grads = masked_grads(bounds_ref, own_ref, other_ref, image).astype(bf16)
+            grad_turned[:, rows] = grads.T
 
     join_cores(core_ref, up_ref, up_swapped_ref, up_whole)
     hidden = dot(second_ref[...], flat(up_whole[...])) + up_add_ref[...]
@@ -275,7 +276,7 @@
     active = (hidden * below).astype(bf16)
     active_ref[...] = active
     slope_ref[...] = (below + hidden * density).astype(bf16)
-    split_cores(core_ref, dot_tn(grad_in[...], active), kept_ref, sent_ref, slice(None))
+    split_cores(core_ref, dot(grad_turned[...], active), kept_ref, sent_ref, slice(None))
 
 
 def dense_down_kernel(opening, *refs):
@@ -287,9 +288,9 @@
     else:
         middle_ref, vec_ref, out_before_ref, back_before_ref = refs[:4]
         kept_ref, sent_ref, up_sums_ref = refs[4:7]
-        out_own_ref, out_other_ref, grad_middle_ref, sums_ref = refs[7:11]
+        out_own_ref, out_other_ref, grad_middle_ref, branch_ref, sums_ref = refs[7:12]
         out_total, back_total = refs[-2:]
-    up_whole, down_whole, grad_in = refs[5:8] if opening else refs[11:14]
+    up_whole, down_whole, grad_in, second_turned = refs[5:9] if opening else refs[12:16]
     step = pl.program_id(0)
     images, slot_count, _ = own_ref.shape
     length = 2 * slot_count
@@ -299,6 +300,7 @@
         for image in range(images):
             rows = slice(image * length, (image + 1) * length)
             grad_in[rows] = masked_grads(bounds_ref, own_ref, other_ref, image).astype(bf16)
+        second_turned[...] = second_ref[...].T
         if opening:
             out_total[...] = jnp.zeros_like(out_total)
             back_total[...] = jnp.zeros_like(back_total)
@@ -311,7 +313,7 @@
     up = flat(up_whole[...])
     down = flat(down_whole[...])
     grad_hidden = (dot(grad_in[...], down) * slope_ref[...].astype(f32)).astype(bf16)
-    split_cores(core_ref, dot_tn(second_ref[...], grad_hidden), kept_ref, sent_ref, slice(None))
+    split_cores(core_ref, dot(second_turned[...], grad_hidden), kept_ref, sent_ref, slice(None))
     up_sums_ref[...] = column_sum(grad_hidden.astype(f32))
     out_total[...] += dot_nt(active_ref[...], down)
     back_total[...] += dot_nt(grad_hidden, up)
@@ -335,6 +337,7 @@
             normal, rate = normal_parts(middle)
             grad_middle = grads + normal_back(normal, rate, vec_ref[3:4], back)
             grad_middle_ref[rows] = grad_middle
+            branch_ref[rows] = grad_middle.astype(bf16)
             for i, term in enumerate((grad_middle, back * normal, back, grads)):
                 sums[i] += column_sum(term)
         for i in range(4):
@@ -403,7 +406,7 @@
 def attend_weights_kernel(
     fsdp,
     core_ref,
-    grad_middle_ref,
+    branch_ref,
     first_ref,
     mixed_ref,
     grad_joint_ref,
@@ -415,11 +418,11 @@
     two_kept_ref,
     two_sent_ref,
 ):
-    total, width = grad_middle_ref.shape
+    total, width = branch_ref.shape
     half = width // 2
     stride = two_kept_ref.shape[-1] // 2
-    first_rows = first_ref[...]
-    branch = grad_middle_ref[...].astype(bf16)
+    first_turned = first_ref[...].T
+    branch_turned = branch_ref[...].T
     for y in range(2):
         at = y * half
         base = y * 2 * half
@@ -431,9 +434,9 @@
             (2, two_kept_ref, two_sent_ref, slice(y * stride, y * stride + half)),
         ):
             start = part * width + at
-            grad = dot_tn(first_rows, grad_joint_ref[:, start : start + half])
+            grad = dot(first_turned, grad_joint_ref[:, start : start + half])
             split_cores(core_ref, grad, kept, sent, columns)
-        grad = dot_tn(branch, mixed_ref[:, at : at + half])
+        grad = dot(branch_turned, mixed_ref[:, at : at + half])
         after = slice(y * stride + half, y * stride + 2 * half)
         split_cores(core_ref, grad, two_kept_ref, two_sent_ref, after)
     each = width // fsdp
@@ -561,7 +564,7 @@
         ],
         input_output_aliases={} if made else {8 + i: i for i in range(6)},
         compiler_params=params(21),
-        cost_estimate=cost(9),
+        cost_estimate=cost(),
         name="attend_forward",
     )(core, bounds, own, other, *one, *two, *([] if made else before), *earlier)
 
@@ -592,9 +595,9 @@
             out(up[0].shape, bf16),
             token,
         ],
-        scratch_shapes=[core_scratch(up[0], tile), pltpu.VMEM((total, width), bf16)],
+        scratch_shapes=[core_scratch(up[0], tile), pltpu.VMEM((width, total), bf16)],
         compiler_params=params(13),
-        cost_estimate=cost(8),
+        cost_estimate=cost(),
         name="dense_up",
     )(core, bounds, second, own, other, *up, up_add, *earlier)
 
@@ -608,16 +611,17 @@
     sums = pl.BlockSpec((8, width), lambda step: (0, 0))
     part_shape = far_out((total, width), f32)
     if opening:
-        more_shapes, more_specs = [part_shape] * 2, [whole] * 2
+        more_shapes, more_specs = [out((total, width), f32)] * 2, [whole] * 2
     else:
-        more_shapes = [out(own.shape, bf16)] * 2 + [part_shape, out((8, width), f32)]
-        more_specs = [fixed(own), fixed(own), whole, sums]
+        more_shapes = [out(own.shape, bf16)] * 2
+        more_shapes += [part_shape, out((total, width), bf16), out((8, width), f32)]
+        more_specs = [fixed(own), fixed(own), whole, whole, sums]
     return pl.pallas_call(
         ordered(
             partial(dense_down_kernel, opening),
             11 if opening else 15,
             len(earlier),
-            3 if opening else 5,
+            4 if opening else 6,
         ),
         grid=(columns // tile,),
         in_specs=[
@@ -644,6 +648,7 @@
             core_scratch(up[0], tile),
             core_scratch(up[0], tile),
             pltpu.VMEM((total, width), bf16),
+            pltpu.VMEM((width, total), bf16),
             *([] if opening else [pltpu.VMEM((total, width), f32)] * 2),
         ],
         compiler_params=params(20 if opening else 31),
@@ -657,7 +662,7 @@
         second,
         active,
         slope,
-        *up,
+        *(in_hbm(array) for array in up),
         *down,
         *([] if opening else before),
         *earlier,
@@ -691,7 +696,7 @@
             *([anywhere] * (len(before) + len(earlier))),
         ],
         out_specs=[block_at((1,) + shape[1:], image) for shape, _ in outs] + [in_smem],
-        out_shape=[far_out(*outs[0])] + [out(*each) for each in outs[1:]] + [token],
+        out_shape=[out(*each) for each in outs] + [token],
         scratch_shapes=[
             core_scratch(one[0]),
             core_scratch(two[0]),
@@ -701,13 +706,13 @@
         compiler_params=params(24),
         cost_estimate=cost(10),
         name="attend_backward",
-    )(core, own, other, grad_middle, joint, chances, *one, *two, vec, *before, *earlier)
+    )(core, own, other, in_hbm(grad_middle), joint, chances, *one, *two, vec, *before, *earlier)
 
 
 def attend_weights(
-    fsdp, core, grad_middle, first, mixed, grad_joint, sums, dense_sums, up_sums, one, two, earlier
+    fsdp, core, branch, first, mixed, grad_joint, sums, dense_sums, up_sums, one, two, earlier
 ):
-    arrays = [core, grad_middle, first, mixed, grad_joint, sums, dense_sums, up_sums]
+    arrays = [core, branch, first, mixed, grad_joint, sums, dense_sums, up_sums]
     outs = [out(pair[0].shape, bf16) for pair in (one, one, two, two)]
     return pl.pallas_call(
         ordered(partial(attend_weights_kernel, fsdp), len(arrays), len(earlier), 0),
@@ -731,6 +736,10 @@
     if kind == "x":
         return (array.shape[0], 2) + array.shape[1:]
     return array.shape[:-1] + (2 * array.shape[-1],)
+
+
+def in_hbm(array):
+    return pltpu.with_memory_space_constraint(array, pltpu.HBM)
 
 
 def take_rows_kernel(side_ref, *refs):
@@ -750,10 +759,10 @@
             out_specs=[pl.BlockSpec(shape, lambda step, side: (0, 0, 0)) for shape in shapes],
         ),
         out_shape=[out(shape, bf16) for shape in shapes],
-        compiler_params=params(8),
+        compiler_params=params(6),
         cost_estimate=cost(),
         name="take_rows",
-    )(side, *arrays)
+    )(side, *(in_hbm(array) for array in arrays))
 
 
 def join_kernel(kinds, places, count, *refs):
@@ -779,7 +788,7 @@
         in_specs=[in_smem] + [in_vmem] * len(arrays) + [anywhere] * len(earlier),
         out_specs=[in_vmem] * len(outs) + [in_smem],
         out_shape=outs + [token],
-        compiler_params=params(24),
+        compiler_params=params(12),
         cost_estimate=cost(),
         name="join_pieces",
     )(sides, *arrays, *earlier)
@@ -800,7 +809,7 @@
         outs[2 + i][...] = passed[i][...]
 
 
-def join_far(sides, blocks, cut_at, passed, earlier):
+def join_far(sides, blocks, cut_at, passed, earlier, microseconds):
     others, rows, columns = blocks[0].shape
     outs = [out((others, 4, rows, size), bf16) for size in (cut_at, columns - cut_at)]
     outs += [out(array.shape, array.dtype) for array in passed]
@@ -809,24 +818,30 @@
         in_specs=[in_smem] + [in_vmem] * (4 + len(passed)) + [anywhere] * len(earlier),
         out_specs=[in_vmem] * len(outs) + [in_smem],
         out_shape=outs + [token],
-        compiler_params=params(24),
-        cost_estimate=cost(),
+        compiler_params=params(12),
+        cost_estimate=cost(microseconds),
         name="join_far",
     )(sides, *blocks, *passed, *earlier)
 
 
-def add_kernel(kinds, places, *refs):
+def add_kernel(kinds, places, count, passing, *refs):
     sides_ref, refs, token_ref = refs[0], refs[1:-1], refs[-1]
     token_ref[0] = 0
     pieces = len(kinds)
-    ins, outs = refs[: 2 * pieces], refs[len(refs) - 2 * pieces :]
+    ins, summed = refs[: 2 * pieces], refs[2 * pieces : 2 * (pieces + count)]
+    passed = refs[2 * (pieces + count) : 2 * (pieces + count) + passing]
+    outs = refs[len(refs) - 2 * pieces - count - passing :]
+    for i in range(count):
+        outs[2 * pieces + i][...] = summed[2 * i][...] + summed[2 * i + 1][...]
+    for i in range(passing):
+        outs[2 * pieces + count + i][...] = passed[i][...]
     for i, kind in enumerate(kinds):
         side = sides_ref[places[i]]
         for at, ref in ((side, outs[2 * i]), (1 - side, outs[2 * i + 1])):
             ref[...] = at_side(ins[2 * i], kind, at)[...] + at_side(ins[2 * i + 1], kind, at)[...]
 
 
-def add_pieces(sides, pieces, kinds, places, earlier, microseconds):
+def add_pieces(sides, pieces, kinds, places, summed, passed, earlier):
     arrays, outs = [], []
     for pair, kind in zip(pieces, kinds):
         for array in pair:
@@ -834,70 +849,93 @@
             arrays.append(array.reshape(blocks // 2, 2, rows, columns) if kind == "x" else array)
         shape = (blocks // 2, rows, columns) if kind == "x" else (blocks, rows, columns // 2)
         outs += [out(shape, bf16)] * 2
+    arrays += [array for pair in summed for array in pair]
+    arrays += passed
+    outs += [out(array.shape, bf16) for array, _ in summed]
+    outs += [out(array.shape, array.dtype) for array in passed]
     outs = pl.pallas_call(
-        partial(add_kernel, kinds, places),
+        partial(add_kernel, kinds, places, len(summed), len(passed)),
         in_specs=[in_smem] + [in_vmem] * len(arrays) + [anywhere] * len(earlier),
         out_specs=[in_vmem] * len(outs) + [in_smem],
         out_shape=outs + [token],
-        compiler_params=params(24),
-        cost_estimate=cost(microseconds),
+        compiler_params=params(12),
+        cost_estimate=cost(),
         name="add_pieces",
     )(sides, *arrays, *earlier)
-    return outs[0:-1:2], outs[1:-1:2], outs[-1]
-
-
-def add_far_kernel(count, *refs):
-    sides_ref, ins, passed, token_ref = refs[0], refs[1:5], refs[5 : 5 + count], refs[-1]
+    count = 2 * len(kinds)
+    return outs[0:count:2], outs[1:count:2], *outs[count:]
+
+
+def add_far_kernel(sizes, count, *refs):
+    sides_ref, token_ref = refs[0], refs[-1]
     token_ref[0] = 0
-    refs = refs[:-1]
-    outs = refs[len(refs) - 4 - count :]
+    ins, passed = refs[1 : 1 + sum(sizes)], refs[1 + sum(sizes) : 1 + sum(sizes) + count]
+    outs = refs[len(refs) - 5 - count : -1]
     place = sides_ref[2]
-    at = 0
-    for kept, arrived in ((ins[0], ins[1]), (ins[2], ins[3])):
-        size = kept.shape[-1]
+    at = first = 0
+    for size in sizes:
+        terms = ins[first : first + size]
+        columns = slice(at, at + terms[0].shape[-1])
         for mask in range(4):
             block = place ^ mask
-            outs[mask][:, :, at : at + size] = kept[:, block] + arrived[:, block]
-        at += size
+            if size == 1:
+                outs[mask][:, :, columns] = terms[0][:, block]
+            else:
+                outs[mask][:, :, columns] = terms[0][:, block] + terms[1][:, block]
+        at, first = columns.stop, first + size
     for i in range(count):
         outs[4 + i][...] = passed[i][...]
 
 
 def add_far(sides, pieces, passed, earlier, microseconds):
     arrays = []
-    for array in (array for pair in pieces for array in pair):
+    for array in (array for piece in pieces for array in piece):
         blocks, rows, columns = array.shape
         arrays.append(array.reshape(blocks // 4, 4, rows, columns))
-    width = pieces[0][0].shape[-1] + pieces[1][0].shape[-1]
+    width = sum(piece[0].shape[-1] for piece in pieces)
     outs = [out((arrays[0].shape[0], rows, width), bf16)] * 4
     outs += [out(array.shape, array.dtype) for array in passed]
+    arrays += passed
     return pl.pallas_call(
-        partial(add_far_kernel, len(passed)),
-        in_specs=[in_smem] + [in_vmem] * (4 + len(passed)) + [anywhere] * len(earlier),
+        partial(add_far_kernel, tuple(len(piece) for piece in pieces), len(passed)),
+        in_specs=[in_smem] + [in_vmem] * len(arrays) + [anywhere] * len(earlier),
         out_specs=[in_vmem] * len(outs) + [in_smem],
         out_shape=outs + [token],
-        compiler_params=params(24),
+        compiler_params=params(12),
         cost_estimate=cost(microseconds),
         name="add_far",
-    )(sides, *arrays, *passed, *earlier)
-
-
-def sum_far_kernel(*refs):
-    total = refs[0][...].astype(f32)
-    for ref in refs[1:4]:
-        total += ref[...].astype(f32)
-    refs[-2][...] = total
+    )(sides, *arrays, *earlier)
+
+
+def sum_far_kernel(cuts, *refs):
+    outs = refs[len(refs) - 1 - len(cuts) : -1]
     refs[-1][0] = 0
-
-
-def sum_far(blocks, earlier):
+    at = 0
+    for (size, form), ref in zip(cuts, outs):
+        total = sum(block[:, :, at : at + size].astype(f32) for block in refs[:4])
+        at += size
+        if form == "parts":
+            parts, _, part = ref.shape
+            for i in range(parts):
+                ref[i] = total[0, :, i * part : (i + 1) * part]
+        else:
+            ref[...] = total
+
+
+def sum_far(blocks, cuts, earlier, microseconds):
+    others, rows, _ = blocks[0].shape
+    shapes = {
+        "whole": lambda size: (others, rows, size),
+        "parts": lambda size: (3, rows, size // 3),
+    }
+    outs = [out(shapes[form](size), f32) for size, form in cuts]
     return pl.pallas_call(
-        sum_far_kernel,
+        partial(sum_far_kernel, cuts),
         in_specs=[in_vmem] * 4 + [anywhere] * len(earlier),
-        out_specs=[in_vmem, in_smem],
-        out_shape=[out(blocks[0].shape, f32), token],
-        compiler_params=params(24),
-        cost_estimate=cost(),
+        out_specs=[in_vmem] * len(outs) + [in_smem],
+        out_shape=outs + [token],
+        compiler_params=params(16),
+        cost_estimate=cost(microseconds),
         name="sum_far",
     )(*blocks, *earlier)
 
@@ -933,8 +971,8 @@
             value = self.spread_bit(value, bit).reshape((-1,) + shard.shape)
         return (value, *(self.swap(value, mask << 2) for mask in (1, 2, 3)))
 
-    def end_far(self, blocks, cut_at, passed=(), earlier=()):
-        *pieces, mark = join_far(self.sides, blocks, cut_at, passed, earlier)
+    def end_far(self, blocks, cut_at, passed=(), earlier=(), microseconds=0.1):
+        *pieces, mark = join_far(self.sides, blocks, cut_at, passed, earlier, microseconds)
         joined = [piece.reshape(-1, self.rows, piece.shape[-1]) for piece in pieces[:2]]
         return joined, pieces[2:], mark
 
@@ -969,9 +1007,9 @@
             sent = lax.dynamic_index_in_dim(whole, 1 - self.side(0), 1, keepdims=False)
         return kept, self.swap(sent, "core")
 
-    def add(self, pairs, kinds, earlier=(), microseconds=0.1):
+    def add(self, pairs, kinds, earlier=(), summed=(), passed=()):
         places = tuple("xy".index(kind) for kind in kinds)
-        return add_pieces(self.sides, pairs, kinds, places, earlier, microseconds)
+        return add_pieces(self.sides, pairs, kinds, places, summed, passed, earlier)
 
     def send(self, kept, sent, kinds):
         return [(value, self.swap(leaving, kind)) for value, leaving, kind in zip(kept, sent, kinds)]
@@ -983,14 +1021,27 @@
     def send_far(self, blocks):
         return (blocks[0], *(self.swap(blocks[mask], mask << 2) for mask in (1, 2, 3)))
 
-    def sum_far(self, blocks, earlier=()):
-        total, mark = sum_far(blocks, earlier)
-        for bit in range(self.bits - 1, 3, -1):
-            total = total.reshape((2, -1) + total.shape[1:])
-            sent = lax.dynamic_index_in_dim(total, 1 - self.side(bit), 0, keepdims=False)
-            kept = lax.dynamic_index_in_dim(total, self.side(bit), 0, keepdims=False)
-            total = kept + self.swap(sent, 1 << bit)
-        return total.reshape(self.rows, -1), mark
+    def sum_far(self, blocks, cuts, earlier=(), microseconds=0.1):
+        if self.bits == 4:
+            *sums, mark = sum_far(blocks, cuts, earlier, microseconds)
+            return [
+                total.reshape(self.rows, -1) if form == "whole" else total.transpose(1, 0, 2)
+                for total, (_, form) in zip(sums, cuts)
+            ], mark
+        plain_cuts = tuple((size, "whole") for size, _ in cuts)
+        *sums, mark = sum_far(blocks, plain_cuts, earlier, microseconds)
+        results = []
+        for total, (size, form) in zip(sums, cuts):
+            for bit in range(self.bits - 1, 3, -1):
+                total = total.reshape((2, -1) + total.shape[1:])
+                sent = lax.dynamic_index_in_dim(total, 1 - self.side(bit), 0, keepdims=False)
+                kept = lax.dynamic_index_in_dim(total, self.side(bit), 0, keepdims=False)
+                total = kept + self.swap(sent, 1 << bit)
+            total = total.reshape(self.rows, size)
+            if form == "parts":
+                total = total.reshape(self.rows, 3, -1)
+            results.append(total)
+        return results, mark
 
 
 def on_device(
@@ -1061,8 +1112,8 @@
     hidden = fsdp * up_bias.shape[0] * 2
     tile = math.gcd(2 * piece, 512)
     attend_blocks = ex.start_far(attend_shard)
-    leaving = take_rows((1 - y).reshape(1), (tokens, cotangent))
-    arriving = [ex.swap(array, "y") for array in leaving]
+    away = (1 - y).reshape(1)
+    arriving = [ex.swap(array, "y") for array in take_rows(away, (tokens, cotangent))]
     pieces, arrived, _ = ex.end_far(attend_blocks, 2 * half, arriving)
     token_rows, grad_rows = (
         (take(array, y * images), other) for array, other in zip((tokens, cotangent), arrived)
@@ -1071,9 +1122,9 @@
     one, two, up_shard, _ = ex.end(pairs, xy, (up_weight,))
     up_blocks = ex.start_far(up_shard)
     pairs = ex.start((one, two), yx)
-    up_pieces, _, mark = ex.end_far(up_blocks, piece)
-    one, two, mark = ex.end(pairs, yx, (), (mark,))
+    one, two, mark = ex.end(pairs, yx)
     one, two = ex.both_cores(one), ex.both_cores(two)
+    up_pieces, _, mark = ex.end_far(up_blocks, piece, (), (mark,), 12)
 
     attend_args = (core, bounds, *token_rows, one, two, fsdp, 2, hidden)
     pairs = ex.start(up_pieces, xy)
@@ -1086,9 +1137,9 @@
     )
     middle = middle.reshape(total, width)
     second = second.reshape(total, width)
-    down_pieces, _, mark = ex.end_far(down_blocks, piece, (), (done,))
-    up_a, up_b, mark = ex.end(pairs, yx, (), (done, mark))
+    up_a, up_b, mark = ex.end(pairs, yx, (), (done,))
     up_a, up_b = ex.both_cores(up_a), ex.both_cores(up_b)
+    down_pieces, _, mark = ex.end_far(down_blocks, piece, (), (mark,), 12)
 
     dense_args = (core, bounds, second, *grad_rows)
     pairs = ex.start(down_pieces, xy)
@@ -1118,6 +1169,7 @@
         out_own,
         out_other,
         grad_middle,
+        branch,
         dense_sums,
         done,
     ) = dense_down(
@@ -1139,21 +1191,18 @@
 
     back_args = (core, *token_rows, grad_middle, joint, chances, one, two, vec)
     *before, done = attend_backward(0, *back_args, [], (mark,))
-    down_blocks, _, mark = ex.add_far(down_pairs, (), (done,))
-    down_blocks = ex.send_far(down_blocks)
-    kept, sent, mark = ex.add(up_pairs, yx, (mark,))
+    kept, sent, *down_sums, mark = ex.add(up_pairs, yx, (done,), down_pairs)
     up_pairs = ex.send(kept, sent, yx)
     grad_joint, grad_own, grad_other, attend_sums, done = attend_backward(
         1, *back_args, before, (mark,)
     )
-    down_grad, mark = ex.sum_far(down_blocks, (done,))
-    kept, sent, mark = ex.add(up_pairs, xy, (mark,))
+    kept, sent, out_other, mark = ex.add(up_pairs, xy, (done,), (), (out_other,))
     up_pairs = ex.send(kept, sent, xy)
     up_sums = jnp.concatenate([up_a_sums, up_b_sums], axis=0)
     one_kept, one_sent, two_kept, two_sent, done = attend_weights(
         fsdp,
         core,
-        grad_middle,
+        branch,
         first_rows.reshape(total, width),
         mixed.reshape(total, width),
         grad_joint.reshape(total, 3 * width),
@@ -1167,27 +1216,29 @@
 
     pairs = [ex.start_cores(one_kept, one_sent), ex.start_cores(two_kept, two_sent)]
     out_back = ex.swap(out_other, "y")
-    up_blocks, (out_back,), mark = ex.add_far(up_pairs, (out_back,), (done,), 12)
-    up_blocks = ex.send_far(up_blocks)
+    dense_blocks, (out_back,), mark = ex.add_far(
+        [*up_pairs, *((array,) for array in down_sums)], (out_back,), (done,), 12
+    )
+    dense_blocks = ex.send_far(dense_blocks)
     kept, sent, mark = ex.add(pairs, yx, (mark,))
     pairs = ex.send(kept, sent, yx)
-    up_grad, mark = ex.sum_far(up_blocks, (mark,))
-    kept, sent, mark = ex.add(pairs, xy, (mark,))
+    kept, sent, mark = ex.add(pairs, xy)
     pairs = ex.send(kept, sent, xy)
-    attend_blocks, (grad_other,), _ = ex.add_far(pairs, (grad_other,))
+    cuts = (2 * piece, "whole"), (2 * piece, "whole")
+    (up_grad, down_grad), mark = ex.sum_far(dense_blocks, cuts, (mark,), 12)
+    attend_blocks, (grad_other,), _ = ex.add_far(pairs, (grad_other,), (mark,))
     attend_blocks = ex.send_far(attend_blocks)
     out_tokens = rows_back(out_own, out_back)
     grad_tokens = rows_back(grad_own, ex.swap(grad_other, "y"))
-    attend_grads, _ = ex.sum_far(attend_blocks, (mark, grad_tokens))
+    cuts = (3 * half, "parts"), (half, "whole"), (128 * len(small), "whole")
+    (grad_qkv, grad_output, small_home), _ = ex.sum_far(attend_blocks, cuts, (mark, grad_tokens))
     small_home = jnp.concatenate(
         [
-            attend_grads[: len(group), 4 * half + block * 128 : 4 * half + (block + 1) * 128]
+            small_home[: len(group), block * 128 : (block + 1) * 128]
             for block, group in enumerate(small_groups(rows))
         ],
         axis=0,
     )
-    grad_qkv = attend_grads[:, : 3 * half].reshape(rows, 3, half)
-    grad_output = attend_grads[:, 3 * half : 4 * half].T
     plain_home = small_home[:6, :rows]
     return (
         out_tokens,
@@ -1196,7 +1247,7 @@
         plain_home[1],
         grad_qkv,
         small_home[6, :rows].reshape(2, rows // 2),
-        grad_output,
+        grad_output.T,
         plain_home[2],
         plain_home[3],
         plain_home[4],

time: 267 us -> 256 us (0.959)
  waiting for transfers between devices: 71.5 us -> 67.3 us
  Pallas kernels: 115 us -> 112 us
    ppermute x42 -> x39, waiting for transfers between devices: 56.6 us -> 41 us  [swap(): lax.ppermute(value, 'fsdp', [(i, i ^ apart) for i in range(self.fsdp)])]
    ppermute x16, waiting for transfers between devices: 15 us -> 26.3 us  [swap(): return lax.ppermute(value, 'tp', [(0, 1), (1, 0)])]
    pallas_call x12 -> x10, Pallas kernels: 19.4 us -> 16.7 us  [the longest x6 10.2 us: add_pieces(): pl.pallas_call(partial(add_kernel, kinds, places, len(summed), len(passed...]
    unnamed x70 -> x74, local copies, waits for them, and re-layouts: 6.64 us -> 4.55 us
    ppermute x42 -> x39, starting transfers between devices: 44.2 us -> 43.1 us  [swap(): lax.ppermute(value, 'fsdp', [(i, i ^ apart) for i in range(self.fsdp)])]
  transfers between devices with their start and end apart: 58 -> 55, of which waited for: 21 -> 20; matrix products, arithmetic and copies ran while one was open for 1% -> 1% of each run, Pallas kernels for 37% -> 38%
where the time goes in v1:
time: 256 us; the launch traced here: 253 us
  Pallas kernels  112 us (44%)
  waiting for transfers between devices  67.3 us (26%)
  starting transfers between devices  61.7 us (24%)
  local copies, waits for them, and re-layouts  7.59 us (3%)
    ppermute x39, starting transfers between devices, swap(): lax.ppermute(value, 'fsdp', [(i, i ^ apart) for i in range(self.fsdp)])  43.1 us
    ppermute x39, waiting for transfers between devices, swap(): lax.ppermute(value, 'fsdp', [(i, i ^ apart) for i in range(self.fsdp)])  41 us
    ppermute x16, waiting for transfers between devices, swap(): return lax.ppermute(value, 'tp', [(0, 1), (1, 0)])  26.3 us
    pallas_call x2, Pallas kernels, dense_down(): pl.pallas_call(ordered(partial(dense_down_kernel, opening), 11 if opening...  22.4 us
    ppermute x16, starting transfers between devices, swap(): return lax.ppermute(value, 'tp', [(0, 1), (1, 0)])  18.6 us
    pallas_call x2, Pallas kernels, attend_forward(): pl.pallas_call(ordered(partial(attend_forward_kernel, image, made, fsdp),...  16.7 us
    pallas_call x2, Pallas kernels, attend_backward(): pl.pallas_call(ordered(attend_backward_kernel, 11 + len(before), len(earl...  16.1 us
    pallas_call x2, Pallas kernels, dense_up(): pl.pallas_call(ordered(dense_up_kernel, 8, len(earlier), 2), grid=(column...  15.5 us
  transfers between devices with their start and end apart: 55, of which 20 were waited for; matrix products, arithmetic and copies ran while one was open for 1% of the time, Pallas kernels for 38%

profile of v1, /device:TPU:0, one launch (start us, length us, event | category | flops | bytes accessed | tf_op | source)
XLA Modules:
  0.0 253.0 jit_solution(3292175419148230733)
XLA Ops:
  2.0 3.0 %collective-permute-start.3 = (bf16[2,128,768]{2,1,0:T(8,128)(2,1)S(1)}, bf16[2,128,768]{2,1,0:T(8,128)(2,1)S(1)}, u32[]{:S(2)}, u32[]{:S(2)}) collective-permute-start(bf16[2,128,768]{2,1,0:T(8,128)(2,1)S(1)} %get-tuple-element.149), channel_id=1, source_target_pairs={{0,1},{1,0},{2,3},{3,2},{4,5},{5,4},{6,7},{7,6},{8,9},{9,8},{10,11... | collective-permute-start | bytes 1179656 | tf_op jit(solution)/shard_map/ppermute | solution.py:959
  5.4 2.1 collective-permute-start
  7.4 2.6 %collective-permute-start.1 = (bf16[1,48,1664]{2,1,0:T(8,128)(2,1)S(1)}, bf16[1,48,1664]{2,1,0:T(8,128)(2,1)S(1)}, u32[]{:S(2)}, u32[]{:S(2)}) collective-permute-start(bf16[1,48,1664]{2,1,0:T(8,128)(2,1)S(1)} %maximum_bitcast_fusion.refs_1_), channel_id=1, source_target_pairs={{0,16},{2,18},{4,20},{6,22},{8,24},{10,26},{12,28},{14,30},{16,0},... | collective-permute-start | bytes 479240 | tf_op jit(solution)/shard_map/ppermute | solution.py:961
  10.1 2.8 %collective-permute-done.refs_2_ = bf16[1,48,1664]{2,1,0:T(8,128)(2,1)S(1)} collective-permute-done((bf16[1,48,1664]{2,1,0:T(8,128)(2,1)S(1)}, bf16[1,48,1664]{2,1,0:T(8,128)(2,1)S(1)}, u32[]{:S(2)}, u32[]{:S(2)}) %collective-permute-start) | collective-permute-done | bytes 159776 | tf_op jit(solution)/shard_map/ppermute | solution.py:961
  12.9 9.0 %collective-permute-done.1.refs_3_ = bf16[1,48,1664]{2,1,0:T(8,128)(2,1)S(1)} collective-permute-done((bf16[1,48,1664]{2,1,0:T(8,128)(2,1)S(1)}, bf16[1,48,1664]{2,1,0:T(8,128)(2,1)S(1)}, u32[]{:S(2)}, u32[]{:S(2)}) %collective-permute-start.1) | collective-permute-done | bytes 159776 | tf_op jit(solution)/shard_map/ppermute | solution.py:961
  27.0 6.1 %collective-permute-done.5.refs_2_ = bf16[4,48,768]{2,1,0:T(8,128)(2,1)S(1)} collective-permute-done((bf16[4,48,768]{2,1,0:T(8,128)(2,1)S(1)}, bf16[4,48,768]{2,1,0:T(8,128)(2,1)S(1)}, u32[]{:S(2)}, u32[]{:S(2)}) %collective-permute-start.5) | collective-permute-done | bytes 294944 | tf_op jit(solution)/shard_map/ppermute | solution.py:961
  40.0 2.6 %collective-permute-start.12 = (bf16[1,48,1536]{2,1,0:T(8,128)(2,1)}, bf16[1,48,1536]{2,1,0:T(8,128)(2,1)}, u32[]{:S(2)}, u32[]{:S(2)}) collective-permute-start(bf16[1,48,1536]{2,1,0:T(8,128)(2,1)} %bitcast.143), channel_id=1, source_target_pairs={{0,16},{2,18},{4,20},{6,22},{8,24},{10,26},{12,28},{14,30},{16,0},... | collective-permute-start | bytes 442376 | tf_op jit(solution)/shard_map/ppermute | solution.py:961
  43.8 5.3 %collective-permute-done.7.refs_2_ = bf16[8,48,768]{2,1,0:T(8,128)(2,1)S(1)} collective-permute-done((bf16[8,48,768]{2,1,0:T(8,128)(2,1)S(1)}, bf16[8,48,768]{2,1,0:T(8,128)(2,1)S(1)}, u32[]{:S(2)}, u32[]{:S(2)}) %collective-permute-start.7) | collective-permute-done | bytes 589856 | tf_op jit(solution)/shard_map/ppermute | solution.py:959
  54.9 2.6 %join_far.4 = (bf16[1,4,48,768]{3,2,1,0:T(8,128)(2,1)}, bf16[1,4,48,768]{3,2,1,0:T(8,128)(2,1)}, s32[1]{0:T(128)}) custom-call(s32[3]{0:T(128)S(1)} %pad_add_fusion.2.refs_0_, bf16[1,48,1536]{2,1,0:T(8,128)(2,1)S(1)} %bitcast.145, bf16[1,48,1536]{2,1,0:T(8,128)(2,1)} %collective-permute-done.11.refs_2_, ...), custom_call_target="tpu_custom_call" | custom-call | flops 12000000000 | bytes 100000 | tf_op jit(solution)/shard_map/join_far/pallas_call | solution.py:816
  61.3 8.9 %attend_forward.2 = (bf16[2,256,768]{2,1,0:T(8,128)(2,1)}, bf16[2,256,2304]{2,1,0:T(8,128)(2,1)}, bf16[2,6,512,256]{3,2,1,0:T(8,128)(2,1)}, bf16[2,256,768]{2,1,...) custom-call(s32[1]{0:T(128)} %bitcast.refs_0_, ...), custom_call_target="tpu_custom_call" | custom-call | flops 100000000 | bytes 100000 | tf_op jit(solution)/shard_map/attend_forward/pallas_call | solution.py:540
  70.3 2.5 join_pieces.8
  75.5 2.6 %collective-permute-start.20 = (bf16[1,48,1536]{2,1,0:T(8,128)(2,1)S(1)}, bf16[1,48,1536]{2,1,0:T(8,128)(2,1)S(1)}, u32[]{:S(2)}, u32[]{:S(2)}) collective-permute-start(bf16[1,48,1536]{2,1,0:T(8,128)(2,1)S(1)} %bitcast.147), channel_id=1, source_target_pairs={{0,16},{2,18},{4,20},{6,22},{8,24},{10,26},{12,28},{14,30},{16,0},... | collective-permute-start | bytes 442376 | tf_op jit(solution)/shard_map/ppermute | solution.py:961
  78.7 7.8 %attend_forward.3 = (bf16[2,256,768]{2,1,0:T(8,128)(2,1)}, bf16[2,256,2304]{2,1,0:T(8,128)(2,1)}, bf16[2,6,512,256]{3,2,1,0:T(8,128)(2,1)}, bf16[2,256,768]{2,1,...) custom-call(s32[1]{0:T(128)} %bitcast.refs_0_, ...), custom_call_target="tpu_custom_call", output_to_operand_aliasing={{0}: (8, {}), {1}: (9, {}), {2}: (10, {}), {3}: (11, {}), {... | custom-call | flops 100000000 | bytes 100000 | tf_op jit(solution)/shard_map/attend_forward/pallas_call | solution.py:540
  94.1 7.6 %dense_up.2 = (bf16[512,1536]{1,0:T(8,128)(2,1)}, bf16[512,1536]{1,0:T(8,128)(2,1)}, bf16[8,48,1536]{2,1,0:T(8,128)(2,1)S(1)}, bf16[8,48,1536]{2,1,0:T(8,128)(2,1)S(1)}, s32[1]{0:T(128)}) custom-call(s32[1]{0:T(128)} %bitcast.refs_0_, s32[2,4]{1,0:T(2,128)S(1)} %pad_add_fusion.1.refs_1_, bf16[512,768]{1,0:T(8,128)(2,1)S(1)} %bitcast.88, ...), custom_call_target="tpu_custom_call" | custom-call | flops 100000000 | bytes 100000 | tf_op jit(solution)/shard_map/dense_up/pallas_call | solution.py:576
  106.0 7.9 %dense_up.3 = (bf16[512,1536]{1,0:T(8,128)(2,1)}, bf16[512,1536]{1,0:T(8,128)(2,1)}, bf16[8,48,1536]{2,1,0:T(8,128)(2,1)S(1)}, bf16[8,48,1536]{2,1,0:T(8,128)(2,1)S(1)}, s32[1]{0:T(128)}) custom-call(s32[1]{0:T(128)} %bitcast.refs_0_, s32[2,4]{1,0:T(2,128)S(1)} %pad_add_fusion.1.refs_1_, bf16[512,768]{1,0:T(8,128)(2,1)S(1)} %bitcast.89, ...), custom_call_target="tpu_custom_call" | custom-call | flops 100000000 | bytes 100000 | tf_op jit(solution)/shard_map/dense_up/pallas_call | solution.py:576
  114.0 4.3 %collective-permute-done.25.refs_2_ = bf16[8,48,768]{2,1,0:T(8,128)(2,1)S(1)} collective-permute-done((bf16[8,48,768]{2,1,0:T(8,128)(2,1)S(1)}, bf16[8,48,768]{2,1,0:T(8,128)(2,1)S(1)}, u32[]{:S(2)}, u32[]{:S(2)}) %collective-permute-start.25) | collective-permute-done | bytes 589856 | tf_op jit(solution)/shard_map/ppermute | solution.py:959
  123.7 9.6 %dense_down.2 = (bf16[8,48,1536]{2,1,0:T(8,128)(2,1)S(1)}, bf16[8,48,1536]{2,1,0:T(8,128)(2,1)S(1)}, f32[1,1536]{1,0:T(1,128)S(1)}, f32[512,768]{1,0:T(8,128)S(1)}, f32[512,768]{1,0:T(8,128)S(1)}, /*index=5*/s32[1]{0:T(128)}) custom-call(s32[1]{0:T(128)} %bitcast.refs_0_, s32[2,4]{1,0:T(2,128)S(1)} %pad_add_fusion.1.refs_1_, ...), custom_call_target="tpu_custom_call" | custom-call | flops 12000000000 | bytes 100000 | tf_op jit(solution)/shard_map/dense_down/pallas_call | solution.py:619
  133.3 1.9 add_pieces.6
  137.9 12.8 %dense_down.3 = (bf16[8,48,1536]{2,1,0:T(8,128)(2,1)S(1)}, bf16[8,48,1536]{2,1,0:T(8,128)(2,1)S(1)}, f32[1,1536]{1,0:T(1,128)S(1)}, bf16[2,128,768]{2,1,0:T(8,12...) custom-call(s32[1]{0:T(128)} %bitcast.refs_0_, ...), custom_call_target="tpu_custom_call" | custom-call | flops 12000000000 | bytes 100000 | tf_op jit(solution)/shard_map/dense_down/pallas_call | solution.py:619
  151.5 1.9 add_pieces.7
  155.4 8.2 %attend_backward.2 = (bf16[2,256,2304]{2,1,0:T(8,128)(2,1)S(1)}, f32[2,128,768]{2,1,0:T(8,128)S(1)}, bf16[2,128,768]{2,1,0:T(8,128)(2,1)S(1)}, f32[2,8,768]{2,1,0:T(8,128)S(1)}, s32[1]{0:T(128)}) custom-call(s32[1]{0:T(128)} %bitcast.refs_0_, bf16[2,128,768]{2,1,0:T(8,128)(2,1)S(1)} %constant_dynamic-slice_fusion.refs_2_.refs_1_, ...), custom_call_target="tpu_custom_call" | custom-call | flops 10000000000 | bytes 100000 | tf_op jit(solution)/shard_map/attend_backward/pallas_call | solution.py:684
  167.6 7.8 %attend_backward.3 = (bf16[2,256,2304]{2,1,0:T(8,128)(2,1)S(1)}, f32[2,128,768]{2,1,0:T(8,128)S(1)}, bf16[2,128,768]{2,1,0:T(8,128)(2,1)S(1)}, f32[2,8,768]{2,1,0:T(8,128)S(1)}, s32[1]{0:T(128)}) custom-call(s32[1]{0:T(128)} %bitcast.refs_0_, ...), custom_call_target="tpu_custom_call", output_to_operand_aliasing={{0}: (11, {}), {1}: (12, {}), {2}: (13, {}), {3}: (14, {})} | custom-call | flops 10000000000 | bytes 100000 | tf_op jit(solution)/shard_map/attend_backward/pallas_call | solution.py:684
  175.4 4.2 %collective-permute-done.37 = bf16[8,48,768]{2,1,0:T(8,128)(2,1)S(1)} collective-permute-done((bf16[8,48,768]{2,1,0:T(8,128)(2,1)S(1)}, bf16[8,48,768]{2,1,0:T(8,128)(2,1)S(1)}, u32[]{:S(2)}, u32[]{:S(2)}) %collective-permute-start.37) | collective-permute-done | bytes 589856 | tf_op jit(solution)/shard_map/ppermute | solution.py:959
  180.5 1.9 add_pieces.9
  186.0 7.9 %attend_weights.1 = (bf16[8,48,1536]{2,1,0:T(8,128)(2,1)S(1)}, bf16[8,48,1536]{2,1,0:T(8,128)(2,1)S(1)}, bf16[8,48,1792]{2,1,0:T(8,128)(2,1)S(1)}, bf16[8,48,1792]{2,1,0:T(8,128)(2,1)S(1)}, s32[1]{0:T(128)}) custom-call(s32[1]{0:T(128)} %bitcast.refs_0_, bf16[512,768]{1,0:T(8,128)(2,1)S(1)} %copy-done.24, bf16[512,768]{1,0:T(8,128)(2,1)S(1)} %bitcast.107, ...), custom_call_target="tpu_custom_call" | custom-call | flops 6000000000 | bytes 100000 | tf_op jit(solution)/shard_map/attend_weights/pallas_call | solution.py:717
  194.5 2.6 %collective-permute-done.40 = bf16[4,48,768]{2,1,0:T(8,128)(2,1)S(1)} collective-permute-done((bf16[4,48,768]{2,1,0:T(8,128)(2,1)S(1)}, bf16[4,48,768]{2,1,0:T(8,128)(2,1)S(1)}, u32[]{:S(2)}, u32[]{:S(2)}) %collective-permute-start.40) | collective-permute-done | bytes 294944 | tf_op jit(solution)/shard_map/ppermute | solution.py:959
  200.5 2.5 collective-permute-start.45
  205.2 2.6 %collective-permute-start.49 = (bf16[1,48,3072]{2,1,0:T(8,128)(2,1)S(1)}, bf16[1,48,3072]{2,1,0:T(8,128)(2,1)S(1)}, u32[]{:S(2)}, u32[]{:S(2)}) collective-permute-start(bf16[1,48,3072]{2,1,0:T(8,128)(2,1)S(1)} %get-tuple-element.270), channel_id=1, source_target_pairs={{0,16},{2,18},{4,20},{6,22},{8,24},{10,26},{12,28},{14,30},{16,0},... | collective-permute-start | bytes 884744 | tf_op jit(solution)/shard_map/ppermute | solution.py:961
  208.0 8.2 %collective-permute-done.44 = bf16[8,48,768]{2,1,0:T(8,128)(2,1)S(1)} collective-permute-done((bf16[8,48,768]{2,1,0:T(8,128)(2,1)S(1)}, bf16[8,48,768]{2,1,0:T(8,128)(2,1)S(1)}, u32[]{:S(2)}, u32[]{:S(2)}) %collective-permute-start.44) | collective-permute-done | bytes 589856 | tf_op jit(solution)/shard_map/ppermute | solution.py:959
  220.7 7.8 %collective-permute-done.49.refs_2_ = bf16[1,48,3072]{2,1,0:T(8,128)(2,1)S(1)} collective-permute-done((bf16[1,48,3072]{2,1,0:T(8,128)(2,1)S(1)}, bf16[1,48,3072]{2,1,0:T(8,128)(2,1)S(1)}, u32[]{:S(2)}, u32[]{:S(2)}) %collective-permute-start.49) | collective-permute-done | bytes 294944 | tf_op jit(solution)/shard_map/ppermute | solution.py:961
  234.0 3.7 %collective-permute-start.52 = (bf16[1,48,1664]{2,1,0:T(8,128)(2,1)S(1)}, bf16[1,48,1664]{2,1,0:T(8,128)(2,1)S(1)}, u32[]{:S(2)}, u32[]{:S(2)}) collective-permute-start(bf16[1,48,1664]{2,1,0:T(8,128)(2,1)S(1)} %get-tuple-element.276), channel_id=1, source_target_pairs={{0,8},{2,10},{4,12},{6,14},{8,0},{10,2},{12,4},{14,6},{16,24},{18,... | collective-permute-start | bytes 479240 | tf_op jit(solution)/shard_map/ppermute | solution.py:961
  241.4 8.4 %collective-permute-done.53.refs_2_ = bf16[1,48,1664]{2,1,0:T(8,128)(2,1)S(1)} collective-permute-done((bf16[1,48,1664]{2,1,0:T(8,128)(2,1)S(1)}, bf16[1,48,1664]{2,1,0:T(8,128)(2,1)S(1)}, u32[]{:S(2)}, u32[]{:S(2)}) %collective-permute-start.53) | collective-permute-done | bytes 159776 | tf_op jit(solution)/shard_map/ppermute | solution.py:961
  (204 shorter events, 81.0 us)
Async XLA Ops:
  2.0 19.9 %collective-permute-start.3 = (bf16[2,128,768]{2,1,0:T(8,128)(2,1)S(1)}, bf16[2,128,768]{2,1,0:T(8,128)(2,1)S(1)}, u32[]{:S(2)}, u32[]{:S(2)}) collective-permute-start(bf16[2,128,768]{2,1,0:T(8,128)(2,1)S(1)} %get-tuple-element.149), channel_id=1, source_target_pairs={{0,1},{1,0},{2,3},{3,2},{4,5},{5,4},{6,7},{7,6},{8,9},{9,8},{10,11... | collective-permute-start | bytes 1179656 | tf_op jit(solution)/shard_map/ppermute | solution.py:959
  5.1 17.5 %collective-permute-start.4 = (bf16[2,128,768]{2,1,0:T(8,128)(2,1)S(1)}, bf16[2,128,768]{2,1,0:T(8,128)(2,1)S(1)}, u32[]{:S(2)}, u32[]{:S(2)}) collective-permute-start(bf16[2,128,768]{2,1,0:T(8,128)(2,1)S(1)} %get-tuple-element.150), channel_id=1, source_target_pairs={{0,1},{1,0},{2,3},{3,2},{4,5},{5,4},{6,7},{7,6},{8,9},{9,8},{10,11... | collective-permute-start | bytes 1179656 | tf_op jit(solution)/shard_map/ppermute | solution.py:959
  7.4 14.5 %collective-permute-start.1 = (bf16[1,48,1664]{2,1,0:T(8,128)(2,1)S(1)}, bf16[1,48,1664]{2,1,0:T(8,128)(2,1)S(1)}, u32[]{:S(2)}, u32[]{:S(2)}) collective-permute-start(bf16[1,48,1664]{2,1,0:T(8,128)(2,1)S(1)} %maximum_bitcast_fusion.refs_1_), channel_id=1, source_target_pairs={{0,16},{2,18},{4,20},{6,22},{8,24},{10,26},{12,28},{14,30},{16,0},... | collective-permute-start | bytes 479240 | tf_op jit(solution)/shard_map/ppermute | solution.py:961
  34.8 15.6 %collective-permute-start.8 = (bf16[4,48,1792]{2,1,0:T(8,128)(2,1)S(1)}, bf16[4,48,1792]{2,1,0:T(8,128)(2,1)S(1)}, u32[]{:S(2)}, u32[]{:S(2)}) collective-permute-start(bf16[4,48,1792]{2,1,0:T(8,128)(2,1)S(1)} %get-tuple-element.156.refs_3_), channel_id=1, source_target_pairs={{0,4},{2,6},{4,0},{6,2},{8,12},{10,14},{12,8},{14,10},{16,20},{18,... | collective-permute-start | bytes 2064392 | tf_op jit(solution)/shard_map/ppermute | solution.py:961
  36.3 12.8 %collective-permute-start.7 = (bf16[8,48,768]{2,1,0:T(8,128)(2,1)S(1)}, bf16[8,48,768]{2,1,0:T(8,128)(2,1)S(1)}, u32[]{:S(2)}, u32[]{:S(2)}) collective-permute-start(bf16[8,48,768]{2,1,0:T(8,128)(2,1)S(1)} %bitcast.113), channel_id=1, source_target_pairs={{0,1},{1,0},{2,3},{3,2},{4,5},{5,4},{6,7},{7,6},{8,9},{9,8},{10,11... | collective-permute-start | bytes 1769480 | tf_op jit(solution)/shard_map/ppermute | solution.py:959
  38.4 16.4 %collective-permute-start.11 = (bf16[1,48,1536]{2,1,0:T(8,128)(2,1)}, bf16[1,48,1536]{2,1,0:T(8,128)(2,1)}, u32[]{:S(2)}, u32[]{:S(2)}) collective-permute-start(bf16[1,48,1536]{2,1,0:T(8,128)(2,1)} %bitcast.142), channel_id=1, source_target_pairs={{0,8},{2,10},{4,12},{6,14},{8,0},{10,2},{12,4},{14,6},{16,24},{18,... | collective-permute-start | bytes 442376 | tf_op jit(solution)/shard_map/ppermute | solution.py:961
  40.0 14.8 %collective-permute-start.12 = (bf16[1,48,1536]{2,1,0:T(8,128)(2,1)}, bf16[1,48,1536]{2,1,0:T(8,128)(2,1)}, u32[]{:S(2)}, u32[]{:S(2)}) collective-permute-start(bf16[1,48,1536]{2,1,0:T(8,128)(2,1)} %bitcast.143), channel_id=1, source_target_pairs={{0,16},{2,18},{4,20},{6,22},{8,24},{10,26},{12,28},{14,30},{16,0},... | collective-permute-start | bytes 442376 | tf_op jit(solution)/shard_map/ppermute | solution.py:961
  42.6 12.2 %collective-permute-start.13 = (bf16[1,48,1536]{2,1,0:T(8,128)(2,1)}, bf16[1,48,1536]{2,1,0:T(8,128)(2,1)}, u32[]{:S(2)}, u32[]{:S(2)}) collective-permute-start(bf16[1,48,1536]{2,1,0:T(8,128)(2,1)} %bitcast.144), channel_id=1, source_target_pairs={{0,24},{2,26},{4,28},{6,30},{8,16},{10,18},{12,20},{14,22},{16,8},... | collective-permute-start | bytes 442376 | tf_op jit(solution)/shard_map/ppermute | solution.py:961
  57.4 12.8 %collective-permute-start.14 = (bf16[4,48,768]{2,1,0:T(8,128)(2,1)}, bf16[4,48,768]{2,1,0:T(8,128)(2,1)}, u32[]{:S(2)}, u32[]{:S(2)}) collective-permute-start(bf16[4,48,768]{2,1,0:T(8,128)(2,1)} %bitcast.22.refs_1_), channel_id=1, source_target_pairs={{0,4},{2,6},{4,0},{6,2},{8,12},{10,14},{12,8},{14,10},{16,20},{18,... | collective-permute-start | bytes 884744 | tf_op jit(solution)/shard_map/ppermute | solution.py:961
  72.8 14.8 %collective-permute-start.16 = (bf16[8,48,768]{2,1,0:T(8,128)(2,1)S(1)}, bf16[8,48,768]{2,1,0:T(8,128)(2,1)S(1)}, u32[]{:S(2)}, u32[]{:S(2)}) collective-permute-start(bf16[8,48,768]{2,1,0:T(8,128)(2,1)S(1)} %bitcast.115), channel_id=1, source_target_pairs={{0,1},{1,0},{2,3},{3,2},{4,5},{5,4},{6,7},{7,6},{8,9},{9,8},{10,11... | collective-permute-start | bytes 1769480 | tf_op jit(solution)/shard_map/ppermute | solution.py:959
  73.4 14.5 %collective-permute-start.17 = (bf16[4,48,1536]{2,1,0:T(8,128)(2,1)S(1)}, bf16[4,48,1536]{2,1,0:T(8,128)(2,1)S(1)}, u32[]{:S(2)}, u32[]{:S(2)}) collective-permute-start(bf16[4,48,1536]{2,1,0:T(8,128)(2,1)S(1)} %get-tuple-element.174.refs_3_), channel_id=1, source_target_pairs={{0,4},{2,6},{4,0},{6,2},{8,12},{10,14},{12,8},{14,10},{16,20},{18,... | collective-permute-start | bytes 1769480 | tf_op jit(solution)/shard_map/ppermute | solution.py:961
  74.3 15.8 %collective-permute-start.19 = (bf16[1,48,1536]{2,1,0:T(8,128)(2,1)S(1)}, bf16[1,48,1536]{2,1,0:T(8,128)(2,1)S(1)}, u32[]{:S(2)}, u32[]{:S(2)}) collective-permute-start(bf16[1,48,1536]{2,1,0:T(8,128)(2,1)S(1)} %bitcast.146), channel_id=1, source_target_pairs={{0,8},{2,10},{4,12},{6,14},{8,0},{10,2},{12,4},{14,6},{16,24},{18,... | collective-permute-start | bytes 442376 | tf_op jit(solution)/shard_map/ppermute | solution.py:961
  75.5 14.7 %collective-permute-start.20 = (bf16[1,48,1536]{2,1,0:T(8,128)(2,1)S(1)}, bf16[1,48,1536]{2,1,0:T(8,128)(2,1)S(1)}, u32[]{:S(2)}, u32[]{:S(2)}) collective-permute-start(bf16[1,48,1536]{2,1,0:T(8,128)(2,1)S(1)} %bitcast.147), channel_id=1, source_target_pairs={{0,16},{2,18},{4,20},{6,22},{8,24},{10,26},{12,28},{14,30},{16,0},... | collective-permute-start | bytes 442376 | tf_op jit(solution)/shard_map/ppermute | solution.py:961
  78.1 12.1 %collective-permute-start.21 = (bf16[1,48,1536]{2,1,0:T(8,128)(2,1)S(1)}, bf16[1,48,1536]{2,1,0:T(8,128)(2,1)S(1)}, u32[]{:S(2)}, u32[]{:S(2)}) collective-permute-start(bf16[1,48,1536]{2,1,0:T(8,128)(2,1)S(1)} %bitcast.148), channel_id=1, source_target_pairs={{0,24},{2,26},{4,28},{6,30},{8,16},{10,18},{12,20},{14,22},{16,8},... | collective-permute-start | bytes 442376 | tf_op jit(solution)/shard_map/ppermute | solution.py:961
  89.6 16.4 %collective-permute-start.18 = (bf16[8,48,1536]{2,1,0:T(8,128)(2,1)S(1)}, bf16[8,48,1536]{2,1,0:T(8,128)(2,1)S(1)}, u32[]{:S(2)}, u32[]{:S(2)}) collective-permute-start(bf16[8,48,1536]{2,1,0:T(8,128)(2,1)S(1)} %bitcast.102), channel_id=1, source_target_pairs={{0,2},{2,0},{4,6},{6,4},{8,10},{10,8},{12,14},{14,12},{16,18},{18,... | collective-permute-start | bytes 3538952 | tf_op jit(solution)/shard_map/ppermute | solution.py:961
  103.5 14.8 %collective-permute-start.25 = (bf16[8,48,768]{2,1,0:T(8,128)(2,1)S(1)}, bf16[8,48,768]{2,1,0:T(8,128)(2,1)S(1)}, u32[]{:S(2)}, u32[]{:S(2)}) collective-permute-start(bf16[8,48,768]{2,1,0:T(8,128)(2,1)S(1)} %bitcast.118), channel_id=1, source_target_pairs={{0,1},{1,0},{2,3},{3,2},{4,5},{5,4},{6,7},{7,6},{8,9},{9,8},{10,11... | collective-permute-start | bytes 1769480 | tf_op jit(solution)/shard_map/ppermute | solution.py:959
  104.5 14.4 %collective-permute-start.26 = (bf16[4,48,1536]{2,1,0:T(8,128)(2,1)S(1)}, bf16[4,48,1536]{2,1,0:T(8,128)(2,1)S(1)}, u32[]{:S(2)}, u32[]{:S(2)}) collective-permute-start(bf16[4,48,1536]{2,1,0:T(8,128)(2,1)S(1)} %get-tuple-element.189.refs_3_), channel_id=1, source_target_pairs={{0,4},{2,6},{4,0},{6,2},{8,12},{10,14},{12,8},{14,10},{16,20},{18,... | collective-permute-start | bytes 1769480 | tf_op jit(solution)/shard_map/ppermute | solution.py:961
  120.8 12.5 %collective-permute-start.30 = (bf16[8,48,1536]{2,1,0:T(8,128)(2,1)S(1)}, bf16[8,48,1536]{2,1,0:T(8,128)(2,1)S(1)}, u32[]{:S(2)}, u32[]{:S(2)}) collective-permute-start(bf16[8,48,1536]{2,1,0:T(8,128)(2,1)S(1)} %get-tuple-element.202), channel_id=1, source_target_pairs={{0,2},{2,0},{4,6},{6,4},{8,10},{10,8},{12,14},{14,12},{16,18},{18,... | collective-permute-start | bytes 3538952 | tf_op jit(solution)/shard_map/ppermute | solution.py:961
  121.4 16.5 %collective-permute-start.27 = (bf16[8,48,1536]{2,1,0:T(8,128)(2,1)S(1)}, bf16[8,48,1536]{2,1,0:T(8,128)(2,1)S(1)}, u32[]{:S(2)}, u32[]{:S(2)}) collective-permute-start(bf16[8,48,1536]{2,1,0:T(8,128)(2,1)S(1)} %bitcast.134), channel_id=1, source_target_pairs={{0,2},{2,0},{4,6},{6,4},{8,10},{10,8},{12,14},{14,12},{16,18},{18,... | collective-permute-start | bytes 3538952 | tf_op jit(solution)/shard_map/ppermute | solution.py:961
  135.2 16.1 %collective-permute-start.33 = (bf16[8,48,768]{2,1,0:T(8,128)(2,1)S(1)}, bf16[8,48,768]{2,1,0:T(8,128)(2,1)S(1)}, u32[]{:S(2)}, u32[]{:S(2)}) collective-permute-start(bf16[8,48,768]{2,1,0:T(8,128)(2,1)S(1)} %get-tuple-element.211), channel_id=1, source_target_pairs={{0,1},{1,0},{2,3},{3,2},{4,5},{5,4},{6,7},{7,6},{8,9},{9,8},{10,11... | collective-permute-start | bytes 1769480 | tf_op jit(solution)/shard_map/ppermute | solution.py:959
  136.4 15.1 %collective-permute-start.34 = (bf16[4,48,1536]{2,1,0:T(8,128)(2,1)S(1)}, bf16[4,48,1536]{2,1,0:T(8,128)(2,1)S(1)}, u32[]{:S(2)}, u32[]{:S(2)}) collective-permute-start(bf16[4,48,1536]{2,1,0:T(8,128)(2,1)S(1)} %get-tuple-element.213), channel_id=1, source_target_pairs={{0,4},{2,6},{4,0},{6,2},{8,12},{10,14},{12,8},{14,10},{16,20},{18,... | collective-permute-start | bytes 1769480 | tf_op jit(solution)/shard_map/ppermute | solution.py:961
  150.7 13.0 %collective-permute-start.32 = (bf16[8,48,1536]{2,1,0:T(8,128)(2,1)S(1)}, bf16[8,48,1536]{2,1,0:T(8,128)(2,1)S(1)}, u32[]{:S(2)}, u32[]{:S(2)}) collective-permute-start(bf16[8,48,1536]{2,1,0:T(8,128)(2,1)S(1)} %get-tuple-element.209), channel_id=1, source_target_pairs={{0,2},{2,0},{4,6},{6,4},{8,10},{10,8},{12,14},{14,12},{16,18},{18,... | collective-permute-start | bytes 3538952 | tf_op jit(solution)/shard_map/ppermute | solution.py:961
  150.8 12.9 %collective-permute-start.31 = (bf16[8,48,1536]{2,1,0:T(8,128)(2,1)S(1)}, bf16[8,48,1536]{2,1,0:T(8,128)(2,1)S(1)}, u32[]{:S(2)}, u32[]{:S(2)}) collective-permute-start(bf16[8,48,1536]{2,1,0:T(8,128)(2,1)S(1)} %get-tuple-element.207), channel_id=1, source_target_pairs={{0,2},{2,0},{4,6},{6,4},{8,10},{10,8},{12,14},{14,12},{16,18},{18,... | collective-permute-start | bytes 3538952 | tf_op jit(solution)/shard_map/ppermute | solution.py:961
  165.5 14.2 %collective-permute-start.37 = (bf16[8,48,768]{2,1,0:T(8,128)(2,1)S(1)}, bf16[8,48,768]{2,1,0:T(8,128)(2,1)S(1)}, u32[]{:S(2)}, u32[]{:S(2)}) collective-permute-start(bf16[8,48,768]{2,1,0:T(8,128)(2,1)S(1)} %get-tuple-element.225), channel_id=1, source_target_pairs={{0,1},{1,0},{2,3},{3,2},{4,5},{5,4},{6,7},{7,6},{8,9},{9,8},{10,11... | collective-permute-start | bytes 1769480 | tf_op jit(solution)/shard_map/ppermute | solution.py:959
  167.0 13.4 %collective-permute-start.38 = (bf16[4,48,1536]{2,1,0:T(8,128)(2,1)S(1)}, bf16[4,48,1536]{2,1,0:T(8,128)(2,1)S(1)}, u32[]{:S(2)}, u32[]{:S(2)}) collective-permute-start(bf16[4,48,1536]{2,1,0:T(8,128)(2,1)S(1)} %get-tuple-element.227), channel_id=1, source_target_pairs={{0,4},{2,6},{4,0},{6,2},{8,12},{10,14},{12,8},{14,10},{16,20},{18,... | collective-permute-start | bytes 1769480 | tf_op jit(solution)/shard_map/ppermute | solution.py:961
  182.4 14.7 %collective-permute-start.41 = (bf16[2,128,768]{2,1,0:T(8,128)(2,1)S(1)}, bf16[2,128,768]{2,1,0:T(8,128)(2,1)S(1)}, u32[]{:S(2)}, u32[]{:S(2)}) collective-permute-start(bf16[2,128,768]{2,1,0:T(8,128)(2,1)S(1)} %get-tuple-element.241), channel_id=1, source_target_pairs={{0,1},{1,0},{2,3},{3,2},{4,5},{5,4},{6,7},{7,6},{8,9},{9,8},{10,11... | collective-permute-start | bytes 1179656 | tf_op jit(solution)/shard_map/ppermute | solution.py:959
  184.4 12.6 %collective-permute-start.40 = (bf16[4,48,768]{2,1,0:T(8,128)(2,1)S(1)}, bf16[4,48,768]{2,1,0:T(8,128)(2,1)S(1)}, u32[]{:S(2)}, u32[]{:S(2)}) collective-permute-start(bf16[4,48,768]{2,1,0:T(8,128)(2,1)S(1)} %get-tuple-element.238), channel_id=1, source_target_pairs={{0,1},{1,0},{2,3},{3,2},{4,5},{5,4},{6,7},{7,6},{8,9},{9,8},{10,11... | collective-permute-start | bytes 884744 | tf_op jit(solution)/shard_map/ppermute | solution.py:959
  200.5 17.5 %collective-permute-start.45 = (bf16[4,48,1792]{2,1,0:T(8,128)(2,1)S(1)}, bf16[4,48,1792]{2,1,0:T(8,128)(2,1)S(1)}, u32[]{:S(2)}, u32[]{:S(2)}) collective-permute-start(bf16[4,48,1792]{2,1,0:T(8,128)(2,1)S(1)} %get-tuple-element.262), channel_id=1, source_target_pairs={{0,4},{2,6},{4,0},{6,2},{8,12},{10,14},{12,8},{14,10},{16,20},{18,... | collective-permute-start | bytes 2064392 | tf_op jit(solution)/shard_map/ppermute | solution.py:961
  203.0 13.1 %collective-permute-start.44 = (bf16[8,48,768]{2,1,0:T(8,128)(2,1)S(1)}, bf16[8,48,768]{2,1,0:T(8,128)(2,1)S(1)}, u32[]{:S(2)}, u32[]{:S(2)}) collective-permute-start(bf16[8,48,768]{2,1,0:T(8,128)(2,1)S(1)} %get-tuple-element.260), channel_id=1, source_target_pairs={{0,1},{1,0},{2,3},{3,2},{4,5},{5,4},{6,7},{7,6},{8,9},{9,8},{10,11... | collective-permute-start | bytes 1769480 | tf_op jit(solution)/shard_map/ppermute | solution.py:959
  203.6 17.1 %collective-permute-start.48 = (bf16[1,48,3072]{2,1,0:T(8,128)(2,1)S(1)}, bf16[1,48,3072]{2,1,0:T(8,128)(2,1)S(1)}, u32[]{:S(2)}, u32[]{:S(2)}) collective-permute-start(bf16[1,48,3072]{2,1,0:T(8,128)(2,1)S(1)} %get-tuple-element.269), channel_id=1, source_target_pairs={{0,8},{2,10},{4,12},{6,14},{8,0},{10,2},{12,4},{14,6},{16,24},{18,... | collective-permute-start | bytes 884744 | tf_op jit(solution)/shard_map/ppermute | solution.py:961
  205.2 23.3 %collective-permute-start.49 = (bf16[1,48,3072]{2,1,0:T(8,128)(2,1)S(1)}, bf16[1,48,3072]{2,1,0:T(8,128)(2,1)S(1)}, u32[]{:S(2)}, u32[]{:S(2)}) collective-permute-start(bf16[1,48,3072]{2,1,0:T(8,128)(2,1)S(1)} %get-tuple-element.270), channel_id=1, source_target_pairs={{0,16},{2,18},{4,20},{6,22},{8,24},{10,26},{12,28},{14,30},{16,0},... | collective-permute-start | bytes 884744 | tf_op jit(solution)/shard_map/ppermute | solution.py:961
  207.8 20.7 %collective-permute-start.50 = (bf16[1,48,3072]{2,1,0:T(8,128)(2,1)S(1)}, bf16[1,48,3072]{2,1,0:T(8,128)(2,1)S(1)}, u32[]{:S(2)}, u32[]{:S(2)}) collective-permute-start(bf16[1,48,3072]{2,1,0:T(8,128)(2,1)S(1)} %get-tuple-element.271), channel_id=1, source_target_pairs={{0,24},{2,26},{4,28},{6,30},{8,16},{10,18},{12,20},{14,22},{16,8},... | collective-permute-start | bytes 884744 | tf_op jit(solution)/shard_map/ppermute | solution.py:961
  (60 other events, 463.2 us)
